TPU v7x, 128 devices: a whole 4x4x4 slice. The times are simulated.
128 devices in a mesh: lat: 16 (over z, x), lon: 8 (over y, core).
Axes of the slice: x: 4, y: 4, z: 4, core: 2. Of those that a mesh axis runs over, the one named last changes fastest.
Arguments:
- grid: bfloat16 [128, 512, 512], P('lat', 'lon'), may hold values from -6 to 6
- mesh_nodes: bfloat16 [16, 8, 256, 512], P('lat', 'lon'), may hold values from -6 to 6
- grid_cot: bfloat16 [128, 512, 512], P('lat', 'lon'), may hold values from -6 to 6
- enc_send: bfloat16 [512, 512], replicated, may hold values from -0.25 to 0.25
- enc_recv: bfloat16 [512, 512], replicated, may hold values from -0.25 to 0.25
- enc_out: bfloat16 [512, 512], replicated, may hold values from -0.25 to 0.25
- dec_send: bfloat16 [512, 512], replicated, may hold values from -0.25 to 0.25
- dec_recv: bfloat16 [512, 512], replicated, may hold values from -0.25 to 0.25
- dec_out: bfloat16 [512, 512], replicated, may hold values from -0.25 to 0.25
- enc_src: int32 [16, 8, 256, 32], P('lat', 'lon'), may hold values from 0 to 65535, as said below
- enc_live: int32 [16, 8, 256, 32], P('lat', 'lon'), may hold values from 0 to 1, as said below
- dec_src: int32 [3, 128, 512], P(None, 'lat', 'lon'), may hold values from 0 to 32767, as said below
Outputs:
- grid_new: bfloat16 [128, 512, 512], P('lat', 'lon')
- grid_grad: bfloat16 [128, 512, 512], P('lat', 'lon')
- mesh_grad: bfloat16 [16, 8, 256, 512], P('lat', 'lon')
- enc_send_grad: float32 [512, 512], replicated
- enc_recv_grad: float32 [512, 512], replicated
- enc_out_grad: float32 [512, 512], replicated
- dec_send_grad: float32 [512, 512], replicated
- dec_recv_grad: float32 [512, 512], replicated
- dec_out_grad: float32 [512, 512], replicated
Inputs may be any that keep to these rules, and one draw needn't show every extreme that they name: `enc_src`: every sender named by the mesh nodes of block (a, b), padded slots included, lies in grid rows a * 8 - 4 to (a + 1) * 8 + 3 and, cyclically, columns b * 64 - 4 to (b + 1) * 64 + 3; these bounds are reached. `enc_live`: the live slots of a mesh node are its first ones, 2 to 32 of them; some node has all 32. `dec_src`: the block (a, b) of every sender of a grid node is at most one block from the node's own block in latitude and, cyclically, in longitude; offsets of one are reached both ways.
All inputs are finite; a program needn't handle non-finite values.
Results may differ from a plain program's by a relative error of at most 0.013.
Values may be sent and summed in bfloat16 or wider, within the bound.
No kernel may reach another device: no remote copies, remote signals or barrier semaphores. Data moves between devices by JAX's collectives and lax.ppermute only.
A program may use at most 192 MiB of HBM per device.

v0:
```python
import jax
import jax.numpy as jnp
from jax import lax
from jax.sharding import PartitionSpec as P

HALO = 4


NORM_EPSILON = 1e-05


def from_behind(shard, axis, by):
    count = lax.axis_size(axis)
    return lax.ppermute(shard, axis, [(i, (i + by) % count) for i in range(count)])


def passed_along(block, axis, distance):
    devices = range(lax.axis_size(axis))
    route = [(i - distance, i) for i in devices if i - distance in devices]
    return lax.ppermute(block, axis, route)


def extended_2(block, sides, width):
    for axis, dim in sides:
        count = lax.axis_size(axis)
        forward = [(i, i + 1) for i in range(count - 1)]
        forward.append((count - 1, 0))
        backward = [(target, source) for source, target in forward]
        low = lax.ppermute(
            lax.slice_in_dim(block, block.shape[dim] - width, None, axis=dim), axis, forward
        )
        high = lax.ppermute(lax.slice_in_dim(block, 0, width, axis=dim), axis, backward)
        block = jnp.concatenate([low, block, high], axis=dim)
    return block


def layer_norm(message):
    centred = message - jnp.mean(message, axis=-1, keepdims=True)
    factor = lax.rsqrt(jnp.mean(centred * centred, axis=-1, keepdims=True) + NORM_EPSILON)
    return (centred * factor, factor)


def edge_forward(senders, node_rows, recv_weight, out_weight, weight_mask, factor):
    receivers, degree, features = senders.shape
    received = jnp.dot(node_rows, recv_weight, preferred_element_type=jnp.float32)
    before = senders + received[:, None, :]
    hidden = jax.nn.silu(before).astype(jnp.bfloat16).reshape(receivers * degree, features)
    message = jnp.dot(hidden, out_weight, preferred_element_type=jnp.float32)
    normed, inverse = layer_norm(message)
    masked = normed.reshape(receivers, degree, features)
    if weight_mask is not None:
        masked = masked * weight_mask[:, :, None]
    summed = jnp.sum(masked, axis=1)
    new_rows = (node_rows.astype(jnp.float32) + factor * summed).astype(jnp.bfloat16)
    return (new_rows, (before, hidden, normed, inverse))


def edge_backward(stored, node_rows, recv_weight, out_weight, weight_mask, factor, node_cot):
    before, hidden, normed, inverse = stored
    receivers, degree, features = before.shape
    spread = jnp.broadcast_to((factor * node_cot)[:, None, :], (receivers, degree, features))
    if weight_mask is not None:
        spread = spread * weight_mask[:, :, None]
    spread = spread.reshape(receivers * degree, features)
    message_cot = inverse * (
        spread
        - jnp.mean(spread, axis=-1, keepdims=True)
        - normed * jnp.mean(spread * normed, axis=-1, keepdims=True)
    )
    message_cot = message_cot.astype(jnp.bfloat16)
    out_grad = jnp.dot(hidden.T, message_cot, preferred_element_type=jnp.float32)
    hidden_cot = jnp.dot(message_cot, out_weight.T, preferred_element_type=jnp.float32)
    hidden_cot = hidden_cot.reshape(receivers, degree, features)
    sigmoid = jax.nn.sigmoid(before)
    before_cot = hidden_cot * sigmoid * (1.0 + before * (1.0 - sigmoid))
    received_cot = jnp.sum(before_cot, axis=1).astype(jnp.bfloat16)
    recv_grad = jnp.dot(node_rows.T, received_cot, preferred_element_type=jnp.float32)
    node_grad = node_cot + jnp.dot(received_cot, recv_weight.T, preferred_element_type=jnp.float32)
    return (before_cot, node_grad, recv_grad, out_grad)


def along_lon(extended, reach):
    inner = extended.shape[1] - 2 * reach
    from_right = from_behind(extended[:, :reach], "lon", -1)
    from_left = from_behind(extended[:, inner + reach :], "lon", 1)
    middle = extended[:, reach : inner + reach]
    middle = middle.at[:, inner - reach :].add(from_right)
    return middle.at[:, :reach].add(from_left)


def along_lat(extended, reach):
    inner = extended.shape[0] - 2 * reach
    from_below = passed_along(extended[:reach], "lat", -1)
    from_above = passed_along(extended[inner + reach :], "lat", 1)
    middle = extended[reach : inner + reach]
    middle = middle.at[inner - reach :].add(from_below)
    return middle.at[:reach].add(from_above)


def fold_back(extended, reach):
    return along_lat(along_lon(extended, reach), reach)


def on_device(
    grid,
    mesh_nodes,
    grid_cot,
    enc_send,
    enc_recv,
    enc_out,
    dec_send,
    dec_recv,
    dec_out,
    enc_src,
    enc_live,
    dec_src,
):
    lat_cells, lon_cells, features = grid.shape
    mesh_slots = mesh_nodes.shape[2]
    degree = enc_src.shape[3]
    lon_count = lax.axis_size("lon")
    lat_index = lax.axis_index("lat")
    lon_index = lax.axis_index("lon")
    reach = HALO
    scaling = degree ** (-0.5)
    lon_total = lon_cells * lon_count
    band_width = lon_cells + 2 * reach
    grid_rows = grid.reshape(lat_cells * lon_cells, features)
    sent = jnp.dot(grid_rows, enc_send, preferred_element_type=jnp.float32).astype(jnp.bfloat16)
    band = extended_2(sent.reshape(lat_cells, lon_cells, features), (("lat", 0), ("lon", 1)), reach)
    band_rows = band.reshape(-1, features)
    source_list = enc_src.reshape(mesh_slots, degree)
    source_row = source_list // lon_total - (lat_index * lat_cells - reach)
    source_col = (source_list % lon_total - lon_index * lon_cells + reach) % lon_total
    local_source = source_row * band_width + source_col
    enc_senders = band_rows[local_source].astype(jnp.float32)
    live = enc_live.reshape(mesh_slots, degree).astype(jnp.float32)
    mesh_rows = mesh_nodes.reshape(mesh_slots, features)
    mesh_new, enc_stored = edge_forward(enc_senders, mesh_rows, enc_recv, enc_out, live, scaling)
    moved = jnp.dot(mesh_new, dec_send, preferred_element_type=jnp.float32).astype(jnp.bfloat16)
    mesh_cycle = extended_2(moved.reshape(1, 1, mesh_slots, features), (("lat", 0), ("lon", 1)), 1)
    cycle_rows = mesh_cycle.reshape(-1, features)
    slot_list = jnp.transpose(dec_src.reshape(3, lat_cells * lon_cells))
    owner = slot_list // mesh_slots
    owner_lat = owner // lon_count - lat_index + 1
    owner_lon = (owner % lon_count - lon_index + 1) % lon_count
    local_slot = (owner_lat * 3 + owner_lon) * mesh_slots + slot_list % mesh_slots
    dec_senders = cycle_rows[local_slot].astype(jnp.float32)
    grid_new, dec_stored = edge_forward(dec_senders, grid_rows, dec_recv, dec_out, None, 1.0)
    cycle_cot, grid_part, dec_recv_grad, dec_out_grad = edge_backward(
        dec_stored,
        grid_rows,
        dec_recv,
        dec_out,
        None,
        1.0,
        grid_cot.reshape(lat_cells * lon_cells, features).astype(jnp.float32),
    )
    cycle_total = jnp.zeros((9 * mesh_slots, features), jnp.float32)
    cycle_total = cycle_total.at[local_slot.reshape(-1)].add(cycle_cot.reshape(-1, features))
    moved_cot = fold_back(cycle_total.reshape(3, 3, mesh_slots, features), 1)
    moved_cot = moved_cot.reshape(mesh_slots, features).astype(jnp.bfloat16)
    dec_send_grad = jnp.dot(mesh_new.T, moved_cot, preferred_element_type=jnp.float32)
    mesh_new_cot = jnp.dot(moved_cot, dec_send.T, preferred_element_type=jnp.float32)
    band_cot, mesh_grad, enc_recv_grad, enc_out_grad = edge_backward(
        enc_stored, mesh_rows, enc_recv, enc_out, live, scaling, mesh_new_cot
    )
    band_total = jnp.zeros(((lat_cells + 2 * reach) * band_width, features), jnp.float32)
    band_total = band_total.at[local_source.reshape(-1)].add(band_cot.reshape(-1, features))
    sent_cot = fold_back(band_total.reshape(lat_cells + 2 * reach, band_width, features), reach)
    sent_cot = sent_cot.reshape(lat_cells * lon_cells, features).astype(jnp.bfloat16)
    enc_send_grad = jnp.dot(grid_rows.T, sent_cot, preferred_element_type=jnp.float32)
    grid_grad = (
        grid_part + jnp.dot(sent_cot, enc_send.T, preferred_element_type=jnp.float32)
    ).astype(jnp.bfloat16)
    enc_send_grad, enc_recv_grad, enc_out_grad, dec_send_grad, dec_recv_grad, dec_out_grad = (
        lax.psum(
            (
                enc_send_grad,
                enc_recv_grad,
                enc_out_grad,
                dec_send_grad,
                dec_recv_grad,
                dec_out_grad,
            ),
            ("lat", "lon"),
        )
    )
    return (
        grid_new.reshape(grid.shape),
        grid_grad.reshape(grid.shape),
        mesh_grad.astype(jnp.bfloat16).reshape(mesh_nodes.shape),
        enc_send_grad,
        enc_recv_grad,
        enc_out_grad,
        dec_send_grad,
        dec_recv_grad,
        dec_out_grad,
    )


def solution(mesh):
    placed = (
        P("lat", "lon", None),
        P("lat", "lon", None, None),
        P("lat", "lon", None),
        P(),
        P(),
        P(),
        P(),
        P(),
        P(),
        P("lat", "lon", None, None),
        P("lat", "lon", None, None),
        P(None, "lat", "lon"),
    )
    return jax.shard_map(
        on_device,
        mesh=mesh,
        in_specs=placed,
        out_specs=(
            P("lat", "lon", None),
            P("lat", "lon", None),
            P("lat", "lon", None, None),
            P(),
            P(),
            P(),
            P(),
            P(),
            P(),
        ),
        check_vma=False,
    )
```

profile of v0, /device:TPU:1, one launch (start us, length us, event | category | flops | bytes accessed | tf_op | source)
XLA Modules:
  0.0 567.3 jit_solution(400389497581327326)
XLA Ops:
  9.0 6.8 %collective-permute-start.1 = (bf16[4,64,512]{2,1,0:T(8,128)(2,1)S(1)}, bf16[4,64,512]{2,1,0:T(8,128)(2,1)S(1)}, u32[]{:S(2)}, u32[]{:S(2)}) collective-permute-start(bf16[4,64,512]{2,1,0:T(8,128)(2,1)S(1)} %bitcast.184), channel_id=1, source_target_pairs={{8,0},{16,8},{24,16},{32,24},{40,32},{48,40},{56,48},{64,56},{72,6... | collective-permute-start | bytes 786440 | tf_op jit(solution)/shard_map/ppermute | solution.py:32
  20.9 5.2 collective-permute-done
  34.6 33.6 %gather_fusion = bf16[8192,512]{1,0:T(8,128)(2,1)} fusion(bf16[1152,512]{1,0:T(8,128)(2,1)S(1)} %bitcast.165, s32[8192]{0:T(1024)S(1)} %broadcast_clamp_fusion), kind=kCustom, calls=%fused_computation | custom fusion | bytes 16809984 | tf_op jit(solution)/shard_map/gather | solution.py:136
  68.1 11.8 %convert_add_fusion = f32[256,32,512]{2,1,0:T(8,128)} fusion(bf16[256,32,512]{2,1,0:T(8,128)(2,1)} %bitcast.167, f32[256,512]{1,0:T(8,128)S(1)} %fusion.47), kind=kLoop, calls=%fused_computation.4 | loop fusion | flops 8388608 | bytes 25690112 | tf_op jit(solution)/shard_map/add | solution.py:46
  79.9 10.6 %fusion.9 = bf16[8192,512]{1,0:T(8,128)(2,1)} fusion(f32[256,32,512]{2,1,0:T(8,128)} %convert_add_fusion), kind=kLoop, calls=%fused_computation.18 | loop fusion | flops 20971520 | bytes 25165824 | tf_op jit(solution)/shard_map/convert_element_type | solution.py:47
  90.6 7.2 %fusion.84 = (f32[8192]{0:T(1024)S(1)}, f32[8192,512]{1,0:T(8,128)S(1)}) fusion(bf16[8192,512]{1,0:T(8,128)(2,1)} %fusion.9, bf16[512,512]{1,0:T(8,128)(2,1)S(1)} %copy-done), kind=kOutput, calls=%fused_computation.178 | convolution fusion | flops 4299153408 | bytes 25722880 | tf_op jit(solution)/shard_map/dot_general | solution.py:48
  101.1 8.3 %multiply_reduce_fusion.2 = (f32[256,512]{1,0:T(8,128)S(1)}, f32[8192,512]{1,0:T(8,128)}) fusion(f32[256,32]{1,0:T(8,128)S(1)} %copy.26, f32[8192]{0:T(1024)S(1)} %add_rsqrt_fusion, f32[8192,512]{1,0:T(8,128)S(1)} %get-tuple-element.182, f32[8192]{0:T(1024)S(1)} %broadcast_multiply_fusion.3), kind=kLoop, calls=%fused_computation.23 | loop fusion | flops 16646144 | bytes 34177024 | tf_op jit(solution)/shard_map/reduce_sum | solution.py:53
  112.5 6.2 %collective-permute-done.5 = bf16[1,1,256,512]{3,2,1,0:T(8,128)(2,1)S(1)} collective-permute-done((bf16[1,1,256,512]{3,2,1,0:T(8,128)(2,1)S(1)}, bf16[1,1,256,512]{3,2,1,0:T(8,128)(2,1)S(1)}, u32[]{:S(2)}, u32[]{:S(2)}) %collective-permute-start.5) | collective-permute-done | bytes 262176 | tf_op jit(solution)/shard_map/ppermute | solution.py:32
  118.7 3.5 collective-permute-done.4
  130.1 6.0 %reshape.803 = f32[1536,512]{1,0:T(8,128)} reshape(f32[512,3,512]{2,1,0:T(4,128)} %broadcast_in_dim.13) | data formatting | bytes 6291456 | tf_op jit(solution)/shard_map/reshape | solution.py:64
  139.3 5.4 gather_fusion.1
  144.7 5.6 reshape.849
  150.3 5.3 broadcast_add_fusion
  155.7 5.9 %add.381 = f32[1536,512]{1,0:T(8,128)} reshape(f32[512,3,512]{2,1,0:T(4,128)} %broadcast_add_fusion) | data formatting | bytes 6291456 | tf_op jit(solution)/shard_map/add | solution.py:46
  174.1 25.9 %scatter_custom_fusion = f32[2304,512]{1,0:T(8,128)} fusion(s32[1536]{0:T(1024)S(1)} %fusion.74, f32[1536,512]{1,0:T(8,128)} %add.381, f32[1536,512]{1,0:T(8,128)} %fusion.87, f32[]{:T(128)} %constant.368.clone.1, f32[]{:T(128)} %constant.367.clone.1), kind=kCustom, calls=%fused_computation.27 | custom fusion | flops 7077888 | bytes 11010056 | tf_op jit(solution)/shard_map/scatter-add | solution.py:160
  200.1 4.1 fusion.78
  207.7 5.8 %reshape.804 = f32[512,3,512]{2,1,0:T(4,128)} reshape(f32[1536,512]{1,0:T(8,128)} %fusion.87) | data formatting | bytes 6291456 | tf_op jit(solution)/shard_map/reshape | solution.py:73
  213.5 7.3 %multiply_reduce_fusion.4 = bf16[512,512]{1,0:T(8,128)(2,1)S(1)} fusion(f32[512,3,512]{2,1,0:T(4,128)} %reshape.804, f32[512,3,512]{2,1,0:T(4,128)} %reshape.849, f32[512,512]{1,0:T(8,128)S(1)} %copy-done.5), kind=kLoop, calls=%fused_computation.26 | loop fusion | flops 7602176 | bytes 7864320 | tf_op jit(solution)/shard_map/reduce_sum | solution.py:76
  220.9 3.8 collective-permute-done.8
  229.1 4.0 collective-permute-start.11
  243.2 7.4 %fusion.5 = f32[8192]{0:T(1024)S(1)} fusion(f32[8192,512]{1,0:T(8,128)} %get-tuple-element.166, f32[8192]{0:T(1024)S(1)} %copy-done.37, f32[256,512]{1,0:T(8,128)S(1)} %get-tuple-element.185), kind=kLoop, calls=%fused_computation.11 | loop fusion | flops 12574720 | bytes 17367040 | tf_op jit(solution)/shard_map/reduce_sum | solution.py:68
  250.7 10.5 %fusion.4 = bf16[8192,512]{1,0:T(8,128)(2,1)} fusion(f32[8192,512]{1,0:T(8,128)} %get-tuple-element.166, f32[8192]{0:T(1024)S(1)} %broadcast_multiply_fusion.2, f32[8192]{0:T(1024)S(1)} %div.118, f32[8192]{0:T(1024)S(1)} %copy-done.37, f32[256,512]{1,0:T(8,128)S(1)} %get-tuple-element.185, f32[8192]{0:T(1024)S(1)} %copy-done.39), kind=kLoop, calls=%fused_computation.10 | loop fusion | flops 25165824 | bytes 25821184 | tf_op jit(solution)/shard_map/convert_element_type | solution.py:70
  261.2 20.3 %fusion.11 = (f32[8192,512]{1,0:T(8,128)}, f32[8192,512]{1,0:T(8,128)}) fusion(f32[256,32,512]{2,1,0:T(8,128)} %convert_add_fusion, bf16[8192,512]{1,0:T(8,128)(2,1)} %fusion.4, bf16[512,512]{1,0:T(8,128)(2,1)S(1)} %copy-done), kind=kOutput, calls=%fused_computation.20 | convolution fusion | flops 4328521728 | bytes 59244544 | tf_op jit(solution)/shard_map/dot_general | solution.py:72
  281.5 12.2 %multiply_reduce_fusion = bf16[256,512]{1,0:T(8,128)(2,1)} fusion(f32[256,512]{1,0:T(8,128)S(1)} %copy-done.13, bf16[8192,512]{1,0:T(8,128)(2,1)} %gather_fusion, f32[8192,512]{1,0:T(8,128)} %get-tuple-element.188), kind=kLoop, calls=%fused_computation.21 | loop fusion | flops 46006272 | bytes 25952256 | tf_op jit(solution)/shard_map/reduce_sum | solution.py:76
  293.7 49.9 %scatter_custom_fusion.1 = f32[1152,512]{1,0:T(8,128)S(1)} fusion(s32[8192]{0:T(1024)} %bitcast.185, f32[8192,512]{1,0:T(8,128)} %get-tuple-element.187, f32[]{:T(128)} %constant.368.clone.1), kind=kCustom, calls=%fused_computation.56 | custom fusion | flops 4194304 | bytes 2359808 | tf_op jit(solution)/shard_map/scatter-add | solution.py:169
  343.7 6.0 %collective-permute-start.12 = (f32[16,4,512]{2,1,0:T(4,128)S(1)}, f32[16,4,512]{2,1,0:T(4,128)S(1)}, u32[]{:S(2)}, u32[]{:S(2)}) collective-permute-start(f32[16,4,512]{2,1,0:T(4,128)S(1)} %get-tuple-element.170), channel_id=1, source_target_pairs={{0,7},{1,0},{2,1},{3,2},{4,3},{5,4},{6,5},{7,6},{8,15},{9,8},{10,9... | collective-permute-start | bytes 393224 | tf_op jit(solution)/shard_map/ppermute | solution.py:14
  349.7 11.2 %fusion.88 = f32[512,512]{1,0:T(8,128)} fusion(bf16[8192,512]{1,0:T(8,128)(2,1)} %fusion.9, bf16[8192,512]{1,0:T(8,128)(2,1)} %fusion.4), kind=kOutput, calls=%fused_computation.182 | convolution fusion | flops 4294967296 | bytes 17825792 | tf_op jit(solution)/shard_map/dot_general | solution.py:71
  362.0 3.6 collective-permute-done.13
  368.4 4.5 collective-permute-start.15
  381.8 5.8 %reshape.802 = f32[512,3,512]{2,1,0:T(4,128)} reshape(f32[1536,512]{1,0:T(8,128)} %copy-done.1) | data formatting | bytes 6291456 | tf_op jit(solution)/shard_map/reshape | solution.py:50
  387.6 4.8 reduce_sum.117
  397.3 150.9 %all-reduce.3.cloned.1.call-done = (f32[512,512]{0,1:T(8,128)}, f32[512,512]{0,1:T(8,128)}, f32[512,512]{1,0:T(8,128)}, f32[512,512]{1,0:T(8,128)}, f32[512,512]{0,1:T(8,128)}, /*index=5*/f32[512,512]{1,0:T(8,128)}) async-done(((f32[512,512]{0,1:T(8,128)}, f32[512,512]{0,1:T(8,128)}, f32[512,512]{1,0:T(8,128)}, f32[512,512]{1,0:T(8,128)}, f32[512,512]{0,1:T(8,128)}, /*index=5*/f32[512,512]{1,0:T(8,128)}), ...) | async-done | bytes 6291472 | tf_op jit(solution)/shard_map/psum | solution.py:177
  (189 shorter events, 92.6 us)
Async XLA Ops:
  7.2 83.4 %copy-start = (bf16[512,512]{1,0:T(8,128)(2,1)S(1)}, bf16[512,512]{1,0:T(8,128)(2,1)}, u32[]{:S(2)}) copy-start(bf16[512,512]{1,0:T(8,128)(2,1)} %param.41) | copy-start | bytes 1572868
  7.2 11.7 %copy-start.16 = (bf16[1,1,256,512]{3,2,1,0:T(8,128)(2,1)S(1)}, bf16[1,1,256,512]{3,2,1,0:T(8,128)(2,1)}, u32[]{:S(2)}) copy-start(bf16[1,1,256,512]{3,2,1,0:T(8,128)(2,1)} %param.37) | copy-start | bytes 786436
  7.2 11.7 %copy-start.28 = (bf16[512,512]{1,0:T(8,128)(2,1)S(1)}, bf16[512,512]{1,0:T(8,128)(2,1)}, u32[]{:S(2)}) copy-start(bf16[512,512]{1,0:T(8,128)(2,1)} %param.40) | copy-start | bytes 1572868
  7.2 540.9 %all-reduce.3.cloned.1.call-start = ((), (), s32[]{:S(2)}) async-start(), calls=%async_computation | async-start | bytes 12582912 | tf_op jit(solution)/shard_map/psum | solution.py:177
  9.0 11.8 %collective-permute-start.1 = (bf16[4,64,512]{2,1,0:T(8,128)(2,1)S(1)}, bf16[4,64,512]{2,1,0:T(8,128)(2,1)S(1)}, u32[]{:S(2)}, u32[]{:S(2)}) collective-permute-start(bf16[4,64,512]{2,1,0:T(8,128)(2,1)S(1)} %bitcast.184), channel_id=1, source_target_pairs={{8,0},{16,8},{24,16},{32,24},{40,32},{48,40},{56,48},{64,56},{72,6... | collective-permute-start | bytes 786440 | tf_op jit(solution)/shard_map/ppermute | solution.py:32
  15.9 10.2 %collective-permute-start = (bf16[4,64,512]{2,1,0:T(8,128)(2,1)S(1)}, bf16[4,64,512]{2,1,0:T(8,128)(2,1)S(1)}, u32[]{:S(2)}, u32[]{:S(2)}) collective-permute-start(bf16[4,64,512]{2,1,0:T(8,128)(2,1)S(1)} %bitcast.183), channel_id=1, source_target_pairs={{0,8},{8,16},{16,24},{24,32},{32,40},{40,48},{48,56},{56,64},{64,7... | collective-permute-start | bytes 786440 | tf_op jit(solution)/shard_map/ppermute | solution.py:29
  19.2 48.9 %copy-start.12 = (f32[256,512]{1,0:T(8,128)}, f32[256,512]{1,0:T(8,128)S(1)}, u32[]{:S(2)}) copy-start(f32[256,512]{1,0:T(8,128)S(1)} %fusion.47) | copy-start | bytes 1572868
  26.1 4.7 collective-permute-start.2
  29.2 3.8 collective-permute-start.3
  101.1 8.4 %copy-start.38 = (f32[8192]{0:T(1024)}, f32[8192]{0:T(1024)S(1)}, u32[]{:S(2)}) copy-start(f32[8192]{0:T(1024)S(1)} %add_rsqrt_fusion) | copy-start | bytes 98308
  101.1 9.1 %copy-start.22 = (bf16[512,512]{1,0:T(8,128)(2,1)S(1)}, bf16[512,512]{1,0:T(8,128)(2,1)}, u32[]{:S(2)}) copy-start(bf16[512,512]{1,0:T(8,128)(2,1)} %param.42) | copy-start | bytes 1572868
  101.1 11.2 %copy-start.10 = (bf16[8,64,512]{2,1,0:T(8,128)(2,1)S(1)}, bf16[8,64,512]{2,1,0:T(8,128)(2,1)}, u32[]{:S(2)}) copy-start(bf16[8,64,512]{2,1,0:T(8,128)(2,1)} %param.38) | copy-start | bytes 1572868
  109.5 15.5 %copy-start.41 = (s32[1,1,256,32]{2,3,1,0:T(8,128)S(1)}, s32[1,1,256,32]{2,3,1,0:T(8,128)}, u32[]{:S(2)}) copy-start(s32[1,1,256,32]{2,3,1,0:T(8,128)} %param.45) | copy-start | bytes 98308
  109.5 16.7 %copy-start.43 = (s32[3,8,64]{2,1,0:T(8,128)S(1)}, s32[3,8,64]{2,1,0:T(8,128)}, u32[]{:S(2)}) copy-start(s32[3,8,64]{2,1,0:T(8,128)} %param.47) | copy-start | bytes 18436
  110.6 8.1 %collective-permute-start.5 = (bf16[1,1,256,512]{3,2,1,0:T(8,128)(2,1)S(1)}, bf16[1,1,256,512]{3,2,1,0:T(8,128)(2,1)S(1)}, u32[]{:S(2)}, u32[]{:S(2)}) collective-permute-start(bf16[1,1,256,512]{3,2,1,0:T(8,128)(2,1)S(1)} %fusion.25), channel_id=1, source_target_pairs={{8,0},{16,8},{24,16},{32,24},{40,32},{48,40},{56,48},{64,56},{72,6... | collective-permute-start | bytes 786440 | tf_op jit(solution)/shard_map/ppermute | solution.py:32
  110.7 11.5 %collective-permute-start.4 = (bf16[1,1,256,512]{3,2,1,0:T(8,128)(2,1)S(1)}, bf16[1,1,256,512]{3,2,1,0:T(8,128)(2,1)S(1)}, u32[]{:S(2)}, u32[]{:S(2)}) collective-permute-start(bf16[1,1,256,512]{3,2,1,0:T(8,128)(2,1)S(1)} %fusion.25), channel_id=1, source_target_pairs={{0,8},{8,16},{16,24},{24,32},{32,40},{40,48},{48,56},{56,64},{64,7... | collective-permute-start | bytes 786440 | tf_op jit(solution)/shard_map/ppermute | solution.py:29
  118.7 8.8 %copy-start.35 = (bf16[1,1,256,512]{3,2,1,0:T(8,128)(2,1)}, bf16[1,1,256,512]{3,2,1,0:T(8,128)(2,1)S(1)}, u32[]{:S(2)}) copy-start(bf16[1,1,256,512]{3,2,1,0:T(8,128)(2,1)S(1)} %collective-permute-done.5) | copy-start | bytes 786436
  123.2 14.4 %collective-permute-start.7 = (bf16[3,1,256,512]{3,2,1,0:T(8,128)(2,1)}, bf16[3,1,256,512]{3,2,1,0:T(8,128)(2,1)}, u32[]{:S(2)}, u32[]{:S(2)}) collective-permute-start(bf16[3,1,256,512]{3,2,1,0:T(8,128)(2,1)} %pad_maximum_fusion.2), channel_id=1, source_target_pairs={{1,0},{2,1},{3,2},{4,3},{5,4},{6,5},{7,6},{0,7},{9,8},{10,9},{11,1... | collective-permute-start | bytes 2359304 | tf_op jit(solution)/shard_map/ppermute | solution.py:32
  124.1 13.5 %collective-permute-start.6 = (bf16[3,1,256,512]{3,2,1,0:T(8,128)(2,1)}, bf16[3,1,256,512]{3,2,1,0:T(8,128)(2,1)}, u32[]{:S(2)}, u32[]{:S(2)}) collective-permute-start(bf16[3,1,256,512]{3,2,1,0:T(8,128)(2,1)} %pad_maximum_fusion.2), channel_id=1, source_target_pairs={{0,1},{1,2},{2,3},{3,4},{4,5},{5,6},{6,7},{7,0},{8,9},{9,10},{10,1... | collective-permute-start | bytes 2359304 | tf_op jit(solution)/shard_map/ppermute | solution.py:29
  204.2 20.5 %collective-permute-start.8 = (f32[3,1,256,512]{3,2,1,0:T(8,128)}, f32[3,1,256,512]{3,2,1,0:T(8,128)}, u32[]{:S(2)}, u32[]{:S(2)}) collective-permute-start(f32[3,1,256,512]{3,2,1,0:T(8,128)} %get-tuple-element.167), channel_id=1, source_target_pairs={{0,7},{1,0},{2,1},{3,2},{4,3},{5,4},{6,5},{7,6},{8,15},{9,8},{10,9... | collective-permute-start | bytes 4718600 | tf_op jit(solution)/shard_map/ppermute | solution.py:14
  205.3 19.3 %collective-permute-start.9 = (f32[3,1,256,512]{3,2,1,0:T(8,128)}, f32[3,1,256,512]{3,2,1,0:T(8,128)}, u32[]{:S(2)}, u32[]{:S(2)}) collective-permute-start(f32[3,1,256,512]{3,2,1,0:T(8,128)} %get-tuple-element.168), channel_id=1, source_target_pairs={{0,1},{1,2},{2,3},{3,4},{4,5},{5,6},{6,7},{7,0},{8,9},{9,10},{10,1... | collective-permute-start | bytes 4718600 | tf_op jit(solution)/shard_map/ppermute | solution.py:14
  220.9 12.2 %copy-start.14 = (bf16[512,512]{1,0:T(8,128)(2,1)}, bf16[512,512]{1,0:T(8,128)(2,1)S(1)}, u32[]{:S(2)}) copy-start(bf16[512,512]{1,0:T(8,128)(2,1)S(1)} %multiply_reduce_fusion.4) | copy-start | bytes 1572868
  220.9 12.2 %copy-start.7 = (bf16[8,64,512]{2,1,0:T(8,128)(2,1)S(1)}, bf16[8,64,512]{2,1,0:T(8,128)(2,1)}, u32[]{:S(2)}) copy-start(bf16[8,64,512]{2,1,0:T(8,128)(2,1)} %param.36) | copy-start | bytes 1572868
  227.6 10.7 %collective-permute-start.10 = (f32[1,1,256,512]{3,2,1,0:T(8,128)S(1)}, f32[1,1,256,512]{3,2,1,0:T(8,128)S(1)}, u32[]{:S(2)}, u32[]{:S(2)}) collective-permute-start(f32[1,1,256,512]{3,2,1,0:T(8,128)S(1)} %get-tuple-element.173), channel_id=1, source_target_pairs={{8,0},{16,8},{24,16},{32,24},{40,32},{48,40},{56,48},{64,56},{72,6... | collective-permute-start | bytes 1572872 | tf_op jit(solution)/shard_map/ppermute | solution.py:20
  229.1 10.1 %collective-permute-start.11 = (f32[1,1,256,512]{3,2,1,0:T(8,128)S(1)}, f32[1,1,256,512]{3,2,1,0:T(8,128)S(1)}, u32[]{:S(2)}, u32[]{:S(2)}) collective-permute-start(f32[1,1,256,512]{3,2,1,0:T(8,128)S(1)} %get-tuple-element.174), channel_id=1, source_target_pairs={{0,8},{8,16},{16,24},{24,32},{32,40},{40,48},{48,56},{56,64},{64,7... | collective-permute-start | bytes 1572872 | tf_op jit(solution)/shard_map/ppermute | solution.py:20
  239.3 11.3 %copy-start.20 = (bf16[256,512]{1,0:T(8,128)(2,1)}, bf16[256,512]{1,0:T(8,128)(2,1)S(1)}, u32[]{:S(2)}) copy-start(bf16[256,512]{1,0:T(8,128)(2,1)S(1)} %fusion.44) | copy-start | bytes 786436
  261.2 20.3 %copy-start.13 = (f32[256,512]{1,0:T(8,128)S(1)}, f32[256,512]{1,0:T(8,128)}, u32[]{:S(2)}) copy-start(f32[256,512]{1,0:T(8,128)} %copy-done.12) | copy-start | bytes 1572868
  343.7 18.3 %collective-permute-start.12 = (f32[16,4,512]{2,1,0:T(4,128)S(1)}, f32[16,4,512]{2,1,0:T(4,128)S(1)}, u32[]{:S(2)}, u32[]{:S(2)}) collective-permute-start(f32[16,4,512]{2,1,0:T(4,128)S(1)} %get-tuple-element.170), channel_id=1, source_target_pairs={{0,7},{1,0},{2,1},{3,2},{4,3},{5,4},{6,5},{7,6},{8,15},{9,8},{10,9... | collective-permute-start | bytes 393224 | tf_op jit(solution)/shard_map/ppermute | solution.py:14
  361.2 11.7 %copy-start.18 = (bf16[256,512]{1,0:T(8,128)(2,1)S(1)}, bf16[256,512]{1,0:T(8,128)(2,1)}, u32[]{:S(2)}) copy-start(bf16[256,512]{1,0:T(8,128)(2,1)} %multiply_reduce_fusion) | copy-start | bytes 786436
  361.2 4.4 collective-permute-start.13
  365.8 11.3 %collective-permute-start.14 = (f32[4,64,512]{2,1,0:T(8,128)S(1)}, f32[4,64,512]{2,1,0:T(8,128)S(1)}, u32[]{:S(2)}, u32[]{:S(2)}) collective-permute-start(f32[4,64,512]{2,1,0:T(8,128)S(1)} %get-tuple-element.172), channel_id=1, source_target_pairs={{8,0},{16,8},{24,16},{32,24},{40,32},{48,40},{56,48},{64,56},{72,6... | collective-permute-start | bytes 1572872 | tf_op jit(solution)/shard_map/ppermute | solution.py:20
  368.4 10.9 %collective-permute-start.15 = (f32[4,64,512]{2,1,0:T(8,128)S(1)}, f32[4,64,512]{2,1,0:T(8,128)S(1)}, u32[]{:S(2)}, u32[]{:S(2)}) collective-permute-start(f32[4,64,512]{2,1,0:T(8,128)S(1)} %get-tuple-element.171), channel_id=1, source_target_pairs={{0,8},{8,16},{16,24},{24,32},{32,40},{40,48},{48,56},{56,64},{64,7... | collective-permute-start | bytes 1572872 | tf_op jit(solution)/shard_map/ppermute | solution.py:20
  (29 other events, 133.7 us)
Sparse Core Ops, SparseCore 0:
  381.9 166.1 all-reduce.2
where the time goes:
time: 576 us; the launch traced here: 567 us
  waiting for transfers between devices  184 us (32%)
  other arithmetic  180 us (31%)
  local copies, waits for them, and re-layouts  96.4 us (17%)
  matrix products  58.5 us (10%)
  starting transfers between devices  33.1 us (6%)
  between operations  15.2 us (3%)
    psum x1, waiting for transfers between devices, on_device(): lax.psum((enc_send_grad, enc_recv_grad, enc_out_grad, dec_send_grad, dec_...  151 us
    scatter-add x1, other arithmetic, on_device(): band_total.at[local_source.reshape(-1)].add(band_cot.reshape(-1, features))  49.9 us
    gather x1, local copies, waits for them, and re-layouts, on_device(): enc_senders = band_rows[local_source].astype(jnp.float32)  33.6 us
    scatter-add x1, other arithmetic, on_device(): cycle_total.at[local_slot.reshape(-1)].add(cycle_cot.reshape(-1, features))  25.9 us
    dot_general x2, matrix products, edge_backward(): jnp.dot(message_cot, out_weight.T, preferred_element_type=jnp.float32)  22.9 us
    reduce_sum x2, other arithmetic, edge_backward(): received_cot = jnp.sum(before_cot, axis=1).astype(jnp.bfloat16)  19.5 us
    add x2, other arithmetic, edge_forward(): before = senders + received[:, None, :]  17.1 us
    unnamed x95, local copies, waits for them, and re-layouts  16.7 us
  transfers between devices with their start and end apart: 17, of which 12 were waited for; matrix products, arithmetic and copies ran while one was open for 12% of the time, Pallas kernels for 0%

commit v1 on v0

v1 whole, which is shorter than its diff:
```python
import jax
import jax.numpy as jnp
from jax import lax
from jax.experimental import pallas as pl
from jax.experimental.pallas import tpu as pltpu
from jax.sharding import PartitionSpec as P

REACH = 4
NORM_EPSILON = 1e-05
BF = jnp.bfloat16
F32 = jnp.float32
VMEM_LIMIT = 56 * 1024 * 1024
ENC_TILE = 32
ENC_CHUNK = 8
DEC_TILE = 128


def dot(a, b):
    return jnp.dot(a, b, preferred_element_type=F32)


def dot_nt(a, b):
    return lax.dot_general(a, b, (((1,), (1,)), ((), ())), preferred_element_type=F32)


def dot_tn(a, b):
    return lax.dot_general(a, b, (((0,), (0,)), ((), ())), preferred_element_type=F32)


def sigma(v):
    return 0.5 * jnp.tanh(0.5 * v) + 0.5


def normalise(message):
    centred = message - jnp.mean(message, axis=-1, keepdims=True)
    factor = lax.rsqrt(jnp.mean(centred * centred, axis=-1, keepdims=True) + NORM_EPSILON)
    return centred, factor


def whole(shape):
    return pl.BlockSpec(shape, lambda t: (0,) * len(shape))


def rows_of(count, width):
    return pl.BlockSpec((count, width), lambda t: (t, 0))


def enc_forward_kernel(
    idx_ref, live_ref, mesh_ref, own_ref, high_ref, low_ref, left_ref, right_ref,
    send_ref, recv_ref, out_ref, dec_send_ref,
    new_ref, moved_ref, before_ref, normed_ref, scale_ref,
    band, onehot,
):
    tile, degree = idx_ref.shape
    width = mesh_ref.shape[1]
    band_rows = band.shape[0]

    @pl.when(pl.program_id(0) == 0)
    def _():
        at = 0
        for piece in (own_ref, high_ref, low_ref, left_ref, right_ref):
            count = piece.shape[0]
            band[at : at + count, :] = dot(piece[...], send_ref[...]).astype(BF)
            at += count

    column = lax.broadcasted_iota(jnp.int32, (tile, band_rows), 1)
    for k in range(degree):
        hit = idx_ref[:, k : k + 1] == column
        onehot[k * tile : (k + 1) * tile, :] = jnp.where(hit, 1.0, 0.0).astype(BF)

    nodes = mesh_ref[...]
    received = dot(nodes, recv_ref[...])
    total = jnp.zeros((tile, width), F32)
    lane = lax.broadcasted_iota(jnp.int32, (tile, degree), 1)
    scales = jnp.zeros((tile, degree), F32)
    rows = ENC_CHUNK * tile
    for c in range(degree // ENC_CHUNK):
        part = pl.ds(c * rows, rows)
        gathered = dot(onehot[part, :], band[...])
        before = gathered.reshape(ENC_CHUNK, tile, width) + received[None]
        before_ref[part, :] = before.reshape(rows, width).astype(BF)
        hidden = (before * sigma(before)).reshape(rows, width).astype(BF)
        centred, factor = normalise(dot(hidden, out_ref[...]))
        normed = (centred * factor).reshape(ENC_CHUNK, tile, width)
        normed_ref[part, :] = normed.reshape(rows, width).astype(BF)
        factor = factor.reshape(ENC_CHUNK, tile, 1)
        for j in range(ENC_CHUNK):
            k = c * ENC_CHUNK + j
            live = live_ref[:, k : k + 1]
            total = total + normed[j] * live
            scales = jnp.where(lane == k, factor[j] * live, scales)
    scale_ref[...] = scales
    new = (nodes.astype(F32) + degree ** (-0.5) * total).astype(BF)
    new_ref[...] = new
    moved_ref[...] = dot(new, dec_send_ref[...]).astype(BF)


def enc_forward(idx, live, mesh_rows, pieces, enc_send, enc_recv, enc_out, dec_send):
    nodes, degree = idx.shape
    width = mesh_rows.shape[1]
    tile = ENC_TILE
    edges = tile * degree
    band_rows = sum(p.shape[0] for p in pieces)
    square = whole((width, width))
    return pl.pallas_call(
        enc_forward_kernel,
        name="enc_forward",
        grid=(nodes // tile,),
        in_specs=[rows_of(tile, degree), rows_of(tile, degree), rows_of(tile, width)]
        + [whole(p.shape) for p in pieces]
        + [square] * 4,
        out_specs=[
            rows_of(tile, width), rows_of(tile, width),
            rows_of(edges, width), rows_of(edges, width), rows_of(tile, degree),
        ],
        out_shape=[
            jax.ShapeDtypeStruct((nodes, width), BF),
            jax.ShapeDtypeStruct((nodes, width), BF),
            jax.ShapeDtypeStruct((nodes * degree, width), BF),
            jax.ShapeDtypeStruct((nodes * degree, width), BF),
            jax.ShapeDtypeStruct((nodes, degree), F32),
        ],
        scratch_shapes=[
            pltpu.VMEM((band_rows, width), BF),
            pltpu.VMEM((edges, band_rows), BF),
        ],
        compiler_params=pltpu.CompilerParams(vmem_limit_bytes=VMEM_LIMIT),
    )(idx, live, mesh_rows, *pieces, enc_send, enc_recv, enc_out, dec_send)


def decoder_kernel(
    idx_ref, idx_row_ref, grid_ref, cot_ref, centre_ref, left_ref, right_ref,
    recv_ref, out_ref,
    new_ref, part_ref, out_grad_ref, recv_grad_ref, centre_tot_ref, left_tot_ref, right_tot_ref,
    onehot, onehot_t, totals, out_acc, recv_acc,
):
    step = pl.program_id(0)
    tile, width = grid_ref.shape
    degree = idx_ref.shape[1]
    cycle = onehot.shape[1]
    third = cycle // 3
    edges = tile * degree

    @pl.when(step == 0)
    def _():
        totals[...] = jnp.zeros_like(totals)
        out_acc[...] = jnp.zeros_like(out_acc)
        recv_acc[...] = jnp.zeros_like(recv_acc)

    column = lax.broadcasted_iota(jnp.int32, (tile, cycle), 1)
    row = lax.broadcasted_iota(jnp.int32, (cycle, tile), 0)
    for j in range(degree):
        hit = idx_ref[:, j : j + 1] == column
        onehot[j * tile : (j + 1) * tile, :] = jnp.where(hit, 1.0, 0.0).astype(BF)
        hit = idx_row_ref[j : j + 1, :] == row
        onehot_t[:, j * tile : (j + 1) * tile] = jnp.where(hit, 1.0, 0.0).astype(BF)

    nodes = grid_ref[...]
    received = dot(nodes, recv_ref[...])
    gathered = dot(onehot[:, :third], centre_ref[...])
    gathered = gathered + dot(onehot[:, third : 2 * third], left_ref[...])
    gathered = gathered + dot(onehot[:, 2 * third :], right_ref[...])
    before = gathered.reshape(degree, tile, width) + received[None]
    sig = sigma(before)
    silu = before * sig
    hidden = silu.reshape(edges, width).astype(BF)
    centred, factor = normalise(dot(hidden, out_ref[...]))
    normed = (centred * factor).reshape(degree, tile, width)
    factor = factor.reshape(degree, tile, 1)
    new_ref[...] = (nodes.astype(F32) + jnp.sum(normed, axis=0)).astype(BF)

    cot = cot_ref[...].astype(F32)
    level = cot - jnp.mean(cot, axis=-1, keepdims=True)
    along = jnp.mean(cot[None] * normed, axis=-1, keepdims=True)
    message_cot = (factor * (level[None] - normed * along)).reshape(edges, width).astype(BF)
    out_acc[...] += dot_tn(hidden, message_cot)
    hidden_cot = dot_nt(message_cot, out_ref[...]).reshape(degree, tile, width)
    before_cot = hidden_cot * (sig + silu * (1.0 - sig))
    received_cot = jnp.sum(before_cot, axis=0).astype(BF)
    recv_acc[...] += dot_tn(nodes, received_cot)
    part_ref[...] = cot + dot_nt(received_cot, recv_ref[...])
    totals[...] += dot(onehot_t[...], before_cot.reshape(edges, width).astype(BF))

    @pl.when(step == pl.num_programs(0) - 1)
    def _():
        out_grad_ref[...] = out_acc[...].astype(BF)
        recv_grad_ref[...] = recv_acc[...].astype(BF)
        centre_tot_ref[...] = totals[:third, :].astype(BF)
        left_tot_ref[...] = totals[third : 2 * third, :].astype(BF)
        right_tot_ref[...] = totals[2 * third :, :].astype(BF)


def decoder(idx, grid_rows, cot_rows, centre, left, right, dec_recv, dec_out):
    nodes, width = grid_rows.shape
    degree = idx.shape[1]
    tile = DEC_TILE
    third = centre.shape[0]
    square = whole((width, width))
    return pl.pallas_call(
        decoder_kernel,
        name="decoder",
        grid=(nodes // tile,),
        in_specs=[
            rows_of(tile, degree),
            pl.BlockSpec((degree, tile), lambda t: (0, t)),
            rows_of(tile, width), rows_of(tile, width),
            whole(centre.shape), whole(centre.shape), whole(centre.shape),
            square, square,
        ],
        out_specs=[
            rows_of(tile, width), rows_of(tile, width), square, square,
            whole(centre.shape), whole(centre.shape), whole(centre.shape),
        ],
        out_shape=[
            jax.ShapeDtypeStruct((nodes, width), BF),
            jax.ShapeDtypeStruct((nodes, width), F32),
            jax.ShapeDtypeStruct((width, width), BF),
            jax.ShapeDtypeStruct((width, width), BF),
            jax.ShapeDtypeStruct(centre.shape, BF),
            jax.ShapeDtypeStruct(centre.shape, BF),
            jax.ShapeDtypeStruct(centre.shape, BF),
        ],
        scratch_shapes=[
            pltpu.VMEM((degree * tile, 3 * third), BF),
            pltpu.VMEM((3 * third, degree * tile), BF),
            pltpu.VMEM((3 * third, width), F32),
            pltpu.VMEM((width, width), F32),
            pltpu.VMEM((width, width), F32),
        ],
        compiler_params=pltpu.CompilerParams(vmem_limit_bytes=VMEM_LIMIT),
    )(idx, idx.T, grid_rows, cot_rows, centre, left, right, dec_recv, dec_out)


def enc_backward_kernel(
    idx_row_ref, scale_ref, mesh_ref, moved_cot_ref, before_ref, normed_ref,
    own_ref, high_ref, low_ref, left_ref, right_ref,
    dec_send_ref, recv_ref, out_ref,
    mesh_grad_ref, band_cot_ref, send_grad_ref, recv_grad_ref, out_grad_ref,
    onehot_t, hidden_all, message_cot_all, before_cot_all, totals, out_acc, recv_acc,
):
    step = pl.program_id(0)
    tile, width = mesh_ref.shape
    degree = scale_ref.shape[1]
    band_rows = totals.shape[0]

    @pl.when(step == 0)
    def _():
        totals[...] = jnp.zeros_like(totals)
        out_acc[...] = jnp.zeros_like(out_acc)
        recv_acc[...] = jnp.zeros_like(recv_acc)

    row = lax.broadcasted_iota(jnp.int32, (band_rows, tile * degree), 0)
    onehot_t[...] = jnp.where(idx_row_ref[0] == row, 1.0, 0.0).astype(BF)

    nodes = mesh_ref[...]
    node_cot = dot_nt(moved_cot_ref[...], dec_send_ref[...])
    spread = degree ** (-0.5) * node_cot
    level = spread - jnp.mean(spread, axis=-1, keepdims=True)
    received_cot = jnp.zeros((tile, width), F32)
    rows = ENC_CHUNK * tile
    for c in range(degree // ENC_CHUNK):
        part = pl.ds(c * rows, rows)
        normed = normed_ref[part, :].astype(F32).reshape(ENC_CHUNK, tile, width)
        along = jnp.mean(spread[None] * normed, axis=-1, keepdims=True)
        message_cot = []
        for j in range(ENC_CHUNK):
            k = c * ENC_CHUNK + j
            scale = scale_ref[:, k : k + 1]
            message_cot.append((scale * (level - normed[j] * along[j])).astype(BF))
        message_cot = jnp.concatenate(message_cot, axis=0)
        message_cot_all[part, :] = message_cot
        before = before_ref[part, :].astype(F32)
        sig = sigma(before)
        silu = before * sig
        hidden_all[part, :] = silu.astype(BF)
        hidden_cot = dot_nt(message_cot, out_ref[...])
        before_cot = hidden_cot * (sig + silu * (1.0 - sig))
        before_cot_all[part, :] = before_cot.astype(BF)
        received_cot = received_cot + jnp.sum(before_cot.reshape(ENC_CHUNK, tile, width), axis=0)
    out_acc[...] += dot_tn(hidden_all[...], message_cot_all[...])
    received_cot = received_cot.astype(BF)
    recv_acc[...] += dot_tn(nodes, received_cot)
    mesh_grad_ref[...] = (node_cot + dot_nt(received_cot, recv_ref[...])).astype(BF)
    totals[...] += dot(onehot_t[...], before_cot_all[...])

    @pl.when(step == pl.num_programs(0) - 1)
    def _():
        out_grad_ref[...] = out_acc[...].astype(BF)
        recv_grad_ref[...] = recv_acc[...].astype(BF)
        band_cot_ref[...] = totals[...].astype(BF)
        at = 0
        send_grad = jnp.zeros((width, width), F32)
        for piece in (own_ref, high_ref, low_ref, left_ref, right_ref):
            count = piece.shape[0]
            send_grad = send_grad + dot_tn(piece[...], band_cot_ref[at : at + count, :])
            at += count
        send_grad_ref[...] = send_grad.astype(BF)


def enc_backward(idx_rows, scale, mesh_rows, moved_cot, before, normed, pieces, dec_send, enc_recv, enc_out):
    nodes, degree = scale.shape
    width = mesh_rows.shape[1]
    tile = ENC_TILE
    edges = tile * degree
    band_rows = sum(p.shape[0] for p in pieces)
    square = whole((width, width))
    return pl.pallas_call(
        enc_backward_kernel,
        name="enc_backward",
        grid=(nodes // tile,),
        in_specs=[
            pl.BlockSpec((1, 1, edges), lambda t: (t, 0, 0)),
            rows_of(tile, degree), rows_of(tile, width), rows_of(tile, width),
            rows_of(edges, width), rows_of(edges, width),
        ]
        + [whole(p.shape) for p in pieces]
        + [square] * 3,
        out_specs=[rows_of(tile, width), whole((band_rows, width)), square, square, square],
        out_shape=[
            jax.ShapeDtypeStruct((nodes, width), BF),
            jax.ShapeDtypeStruct((band_rows, width), BF),
            jax.ShapeDtypeStruct((width, width), BF),
            jax.ShapeDtypeStruct((width, width), BF),
            jax.ShapeDtypeStruct((width, width), BF),
        ],
        scratch_shapes=[
            pltpu.VMEM((band_rows, edges), BF),
            pltpu.VMEM((edges, width), BF),
            pltpu.VMEM((edges, width), BF),
            pltpu.VMEM((edges, width), BF),
            pltpu.VMEM((band_rows, width), F32),
            pltpu.VMEM((width, width), F32),
            pltpu.VMEM((width, width), F32),
        ],
        compiler_params=pltpu.CompilerParams(vmem_limit_bytes=VMEM_LIMIT),
    )(idx_rows, scale, mesh_rows, moved_cot, before, normed, *pieces, dec_send, enc_recv, enc_out)


def to_lon(shard, by):
    count = lax.axis_size("lon")
    return lax.ppermute(shard, "lon", [(i, (i + by) % count) for i in range(count)])


def to_lat(shard, by):
    count = lax.axis_size("lat")
    return lax.ppermute(shard, "lat", [(i, i + by) for i in range(count) if 0 <= i + by < count])


def summed_everywhere(stack):
    axes = ("lat", "lon")
    lon_count = lax.axis_size("lon")
    count = lax.axis_size("lat") * lon_count
    rows, width = stack.shape
    half = rows // 2
    core = lax.axis_index("lon") % 2
    swap = [(i, i ^ 1) for i in range(lon_count)]
    alike = [[i for i in range(count) if i % 2 == c] for c in range(2)]
    kept = lax.dynamic_slice_in_dim(stack, core * half, half, 0).astype(F32)
    given = lax.dynamic_slice_in_dim(stack, (1 - core) * half, half, 0)
    kept = kept + lax.ppermute(given, "lon", swap).astype(F32)
    parts = kept.astype(BF).reshape(count // 2, 2 * half // count, width)
    got = lax.all_to_all(parts, axes, 0, 0, axis_index_groups=alike, tiled=True)
    mine = jnp.sum(got.astype(F32), axis=0).astype(BF)
    spread = jnp.broadcast_to(mine[None], parts.shape)
    ours = lax.all_to_all(spread, axes, 0, 0, axis_index_groups=alike, tiled=True).reshape(half, width)
    theirs = lax.ppermute(ours, "lon", swap)
    first = jnp.where(core == 0, ours, theirs).astype(F32)
    second = jnp.where(core == 0, theirs, ours).astype(F32)
    return first, second


def on_device(
    grid, mesh_nodes, grid_cot, enc_send, enc_recv, enc_out, dec_send, dec_recv, dec_out,
    enc_src, enc_live, dec_src,
):
    lat_cells, lon_cells, width = grid.shape
    slots, degree = enc_src.shape[2:]
    lat_index = lax.axis_index("lat")
    lon_index = lax.axis_index("lon")
    lon_count = lax.axis_size("lon")
    lon_total = lon_cells * lon_count
    cells = lat_cells * lon_cells
    edge_rows = REACH * lon_cells
    tall = lat_cells + 2 * REACH

    grid_rows = grid.reshape(cells, width)
    mesh_rows = mesh_nodes.reshape(slots, width)
    high = to_lat(grid_rows[:edge_rows], -1)
    low = to_lat(grid_rows[cells - edge_rows :], 1)
    inner = jnp.concatenate([grid_rows, high, low], axis=0).reshape(tall, lon_cells, width)
    left = to_lon(inner[:, lon_cells - REACH :].reshape(tall * REACH, width), 1)
    right = to_lon(inner[:, :REACH].reshape(tall * REACH, width), -1)
    pieces = (grid_rows, high, low, left, right)

    source = enc_src.reshape(slots, degree)
    row = (source // lon_total - lat_index * lat_cells) % tall
    col = (source % lon_total - lon_index * lon_cells + REACH) % lon_total - REACH
    inner_rows = tall * lon_cells
    enc_idx = jnp.where(
        col < 0,
        inner_rows + row * REACH + col + REACH,
        jnp.where(
            col >= lon_cells,
            inner_rows + tall * REACH + row * REACH + col - lon_cells,
            row * lon_cells + col,
        ),
    )
    tiles = slots // ENC_TILE
    enc_idx_rows = enc_idx.reshape(tiles, ENC_TILE, degree).transpose(0, 2, 1)
    enc_idx_rows = enc_idx_rows.reshape(tiles, 1, ENC_TILE * degree)
    live = enc_live.reshape(slots, degree).astype(F32)

    picks = dec_src.reshape(3, cells).T
    owner = picks // slots
    owner_lat = (owner // lon_count - lat_index) % 3
    owner_lon = (owner % lon_count - lon_index + lon_count) % lon_count
    owner_lon = jnp.where(owner_lon == lon_count - 1, 1, owner_lon * 2)
    dec_idx = (owner_lon * 3 + owner_lat) * slots + picks % slots

    mesh_new, moved, before, normed, scale = enc_forward(
        enc_idx, live, mesh_rows, pieces, enc_send, enc_recv, enc_out, dec_send
    )

    above = to_lat(moved, -1)
    below = to_lat(moved, 1)
    centre = jnp.concatenate([moved, above, below], axis=0)
    west = to_lon(centre, 1)
    east = to_lon(centre, -1)
    grid_new, grid_part, dec_out_grad, dec_recv_grad, centre_tot, west_tot, east_tot = decoder(
        dec_idx, grid_rows, grid_cot.reshape(cells, width), centre, west, east, dec_recv, dec_out
    )
    from_east = to_lon(west_tot, -1)
    from_west = to_lon(east_tot, 1)
    column = centre_tot.astype(F32) + from_east.astype(F32) + from_west.astype(F32)
    from_below = to_lat(column[slots : 2 * slots].astype(BF), 1)
    from_above = to_lat(column[2 * slots :].astype(BF), -1)
    moved_cot = column[:slots] + from_below.astype(F32) + from_above.astype(F32)
    moved_cot = moved_cot.astype(BF)
    dec_send_grad = dot_tn(mesh_new, moved_cot).astype(BF)

    mesh_grad, band_cot, enc_send_grad, enc_recv_grad, enc_out_grad = enc_backward(
        enc_idx_rows, scale, mesh_rows, moved_cot, before, normed, pieces, dec_send, enc_recv, enc_out
    )
    enc_grads, dec_grads = summed_everywhere(
        jnp.concatenate(
            [enc_send_grad, enc_recv_grad, enc_out_grad, dec_send_grad, dec_recv_grad, dec_out_grad], axis=0
        )
    )

    side = tall * REACH
    from_right = to_lon(band_cot[inner_rows : inner_rows + side], -1)
    from_left = to_lon(band_cot[inner_rows + side :], 1)
    inner_cot = band_cot[:inner_rows].astype(F32).reshape(tall, lon_cells, width)
    inner_cot = inner_cot.at[:, lon_cells - REACH :].add(from_right.astype(F32).reshape(tall, REACH, width))
    inner_cot = inner_cot.at[:, :REACH].add(from_left.astype(F32).reshape(tall, REACH, width))
    inner_cot = inner_cot.reshape(inner_rows, width)
    from_low = to_lat(inner_cot[cells : cells + edge_rows].astype(BF), 1)
    from_high = to_lat(inner_cot[cells + edge_rows :].astype(BF), -1)
    sent_cot = inner_cot[:cells] + jnp.concatenate([from_low, from_high], axis=0).astype(F32)
    grid_grad = (grid_part + dot_nt(sent_cot.astype(BF), enc_send)).astype(BF)

    return (
        grid_new.reshape(grid.shape),
        grid_grad.reshape(grid.shape),
        mesh_grad.reshape(mesh_nodes.shape),
        enc_grads[:width],
        enc_grads[width : 2 * width],
        enc_grads[2 * width :],
        dec_grads[:width],
        dec_grads[width : 2 * width],
        dec_grads[2 * width :],
    )


def solution(mesh):
    node = P("lat", "lon", None)
    block = P("lat", "lon", None, None)
    placed = (
        node, block, node, P(), P(), P(), P(), P(), P(), block, block, P(None, "lat", "lon"),
    )
    return jax.shard_map(
        on_device,
        mesh=mesh,
        in_specs=placed,
        out_specs=(node, node, block, P(), P(), P(), P(), P(), P()),
        check_vma=False,
    )
```

time: 576 us -> 272 us (0.47); the launches traced: 567 us -> 270 us
  other arithmetic: 180 us -> 12.2 us
  waiting for transfers between devices: 184 us -> 64.4 us
  Pallas kernels: 0 us -> 92.1 us
  local copies, waits for them, and re-layouts: 96.4 us -> 15.3 us
  matrix products: 58.5 us -> 0.79 us
  blocking collectives: 0 us -> 39.2 us
  between operations: 15.2 us -> 1.1 us
  starting transfers between devices: 33.1 us -> 45.1 us
    psum x1 -> x0, waiting for transfers between devices: 151 us -> none  [on_device(): lax.psum((enc_send_grad, enc_recv_grad, enc_out_grad, dec_send_grad, dec_...]
    pallas_call x0 -> x3, Pallas kernels: none -> 92.1 us  [the longest x1 40.7 us: enc_backward(): pl.pallas_call(enc_backward_kernel, name='enc_backward', grid=(nodes // t...]
    scatter-add x6 -> x2, other arithmetic: 76.2 us -> 0.12 us  [the longest x1 0.07 us: on_device(): inner_cot.at[:, lon_cells - REACH:]]
    dot_general x18 -> x2, matrix products: 58.5 us -> 0.79 us  [the longest x1 0.46 us: dot_nt(): lax.dot_general(a, b, (((1,), (1,)), ((), ())), preferred_element_type=F32)]
    reduce_sum x10 -> x1, other arithmetic: 47.9 us -> 0.23 us  [summed_everywhere(): mine = jnp.sum(got.astype(F32), axis=0).astype(BF)]
    all_to_all x0 -> x1, blocking collectives: none -> 39.2 us  [summed_everywhere(): got = lax.all_to_all(parts, axes, 0, 0, axis_index_groups=alike, tiled=True)]
    gather x2 -> x0, local copies, waits for them, and re-layouts: 39 us -> none  [the longest x1 33.6 us: on_device(): enc_senders = band_rows[local_source].astype(jnp.float32)]
    ppermute x16 -> x18, waiting for transfers between devices: 33.6 us -> 59.9 us  [the longest x8 36.1 us: to_lon(): lax.ppermute(shard, 'lon', [(i, (i + by) % count) for i in range(count)])]
  transfers between devices with their start and end apart: 17 -> 19, of which waited for: 12 -> 16; matrix products, arithmetic and copies ran while one was open for 12% -> 4% of each run, Pallas kernels for 0% -> 0%
where the time goes in v1:
time: 272 us; the launch traced here: 270 us
  Pallas kernels  92.1 us (34%)
  waiting for transfers between devices  64.4 us (24%)
  starting transfers between devices  45.1 us (17%)
  blocking collectives  39.2 us (14%)
  local copies, waits for them, and re-layouts  15.3 us (6%)
  other arithmetic  12.2 us (4%)
    pallas_call x1, Pallas kernels, enc_backward(): pl.pallas_call(enc_backward_kernel, name='enc_backward', grid=(nodes // t...  40.7 us
    all_to_all x1, blocking collectives, summed_everywhere(): got = lax.all_to_all(parts, axes, 0, 0, axis_index_groups=alike, tiled=True)  39.2 us
    ppermute x8, waiting for transfers between devices, to_lon(): lax.ppermute(shard, 'lon', [(i, (i + by) % count) for i in range(count)])  36.1 us
    pallas_call x1, Pallas kernels, enc_forward(): pl.pallas_call(enc_forward_kernel, name='enc_forward', grid=(nodes // til...  29.8 us
    pallas_call x1, Pallas kernels, decoder(): pl.pallas_call(decoder_kernel, name='decoder', grid=(nodes // tile,), in_...  21.6 us
    ppermute x8, starting transfers between devices, to_lat(): lax.ppermute(shard, 'lat', [(i, i + by) for i in range(count) if 0 <= i +...  20.9 us
    ppermute x8, waiting for transfers between devices, to_lat(): lax.ppermute(shard, 'lat', [(i, i + by) for i in range(count) if 0 <= i +...  20.4 us
    ppermute x8, starting transfers between devices, to_lon(): lax.ppermute(shard, 'lon', [(i, (i + by) % count) for i in range(count)])  9.26 us
  transfers between devices with their start and end apart: 19, of which 16 were waited for; matrix products, arithmetic and copies ran while one was open for 4% of the time, Pallas kernels for 0%

profile of v1, /device:TPU:1, one launch (start us, length us, event | category | flops | bytes accessed | tf_op | source)
XLA Modules:
  0.0 270.2 jit_solution(7579923671932468454)
XLA Ops:
  1.7 1.3 collective-permute-start
  3.0 4.6 %collective-permute-start.1 = (bf16[256,512]{1,0:T(8,128)(2,1)S(1)}, bf16[256,512]{1,0:T(8,128)(2,1)S(1)}, u32[]{:S(2)}, u32[]{:S(2)}) collective-permute-start(bf16[256,512]{1,0:T(8,128)(2,1)S(1)} %bitcast.80), channel_id=1, source_target_pairs={{0,8},{8,16},{16,24},{24,32},{32,40},{40,48},{48,56},{56,64},{64,7... | collective-permute-start | bytes 786440 | tf_op jit(solution)/shard_map/ppermute | solution.py:346
  13.4 3.5 %collective-permute-start.2 = (bf16[64,512]{1,0:T(8,128)(2,1)S(1)}, bf16[64,512]{1,0:T(8,128)(2,1)S(1)}, u32[]{:S(2)}, u32[]{:S(2)}) collective-permute-start(bf16[64,512]{1,0:T(8,128)(2,1)S(1)} %reshape.155), channel_id=1, source_target_pairs={{0,1},{1,2},{2,3},{3,4},{4,5},{5,6},{6,7},{7,0},{8,9},{9,10},{10,1... | collective-permute-start | bytes 196616 | tf_op jit(solution)/shard_map/ppermute | solution.py:341
  18.2 2.4 collective-permute-done.3.right_ref
  21.2 29.8 %enc_forward.1 = (bf16[256,512]{1,0:T(8,128)(2,1)}, bf16[256,512]{1,0:T(8,128)(2,1)}, bf16[8192,512]{1,0:T(8,128)(2,1)}, bf16[8192,512]{1,0:T(8,128)(2,1)}, f32[256,32]{1,0:T(8,128)}) custom-call(s32[256,32]{1,0:T(8,128)} %select_select_fusion.idx_ref, f32[256,32]{1,0:T(8,128)} %convert_bitcast_fusion.live_ref, bf16[256,512]{1,0:T(8,128)(2,1)} %bitcast.76, ...), custom_call_target="tpu_custom_call" | custom-call | tf_op jit(solution)/shard_map/enc_forward/pallas_call | solution.py:105
  51.0 1.3 collective-permute-start.4
  52.3 4.8 %collective-permute-start.5 = (bf16[256,512]{1,0:T(8,128)(2,1)}, bf16[256,512]{1,0:T(8,128)(2,1)S(1)}, u32[]{:S(2)}, u32[]{:S(2)}) collective-permute-start(bf16[256,512]{1,0:T(8,128)(2,1)} %get-tuple-element.50), channel_id=1, source_target_pairs={{0,8},{8,16},{16,24},{24,32},{32,40},{40,48},{48,56},{56,64},{64,7... | collective-permute-start | bytes 786440 | tf_op jit(solution)/shard_map/ppermute | solution.py:346
  58.1 4.0 %collective-permute-done.4 = bf16[256,512]{1,0:T(8,128)(2,1)S(1)} collective-permute-done((bf16[256,512]{1,0:T(8,128)(2,1)}, bf16[256,512]{1,0:T(8,128)(2,1)S(1)}, u32[]{:S(2)}, u32[]{:S(2)}) %collective-permute-start.4) | collective-permute-done | bytes 262176 | tf_op jit(solution)/shard_map/ppermute | solution.py:346
  65.6 7.0 %collective-permute-done.6.left_ref = bf16[768,512]{1,0:T(8,128)(2,1)S(1)} collective-permute-done((bf16[768,512]{1,0:T(8,128)(2,1)S(1)}, bf16[768,512]{1,0:T(8,128)(2,1)S(1)}, u32[]{:S(2)}, u32[]{:S(2)}) %collective-permute-start.6) | collective-permute-done | bytes 786464 | tf_op jit(solution)/shard_map/ppermute | solution.py:341
  72.6 2.8 %collective-permute-done.7.right_ref = bf16[768,512]{1,0:T(8,128)(2,1)S(1)} collective-permute-done((bf16[768,512]{1,0:T(8,128)(2,1)S(1)}, bf16[768,512]{1,0:T(8,128)(2,1)S(1)}, u32[]{:S(2)}, u32[]{:S(2)}) %collective-permute-start.7) | collective-permute-done | bytes 786464 | tf_op jit(solution)/shard_map/ppermute | solution.py:341
  76.3 21.6 %decoder.1 = (bf16[512,512]{1,0:T(8,128)(2,1)}, f32[512,512]{1,0:T(8,128)}, bf16[512,512]{1,0:T(8,128)(2,1)}, bf16[512,512]{1,0:T(8,128)(2,1)}, bf16[768,512]{1,...) custom-call(s32[512,3]{1,0:T(8,128)} %copy.23.idx_ref, s32[3,512]{1,0:T(4,128)} %fusion.38.idx_row_ref, ...), custom_call_target="tpu_custom_call" | custom-call | tf_op jit(solution)/shard_map/decoder/pallas_call | solution.py:199
  97.9 1.4 collective-permute-start.8
  99.6 10.2 %collective-permute-done.8 = bf16[768,512]{1,0:T(8,128)(2,1)S(1)} collective-permute-done((bf16[768,512]{1,0:T(8,128)(2,1)}, bf16[768,512]{1,0:T(8,128)(2,1)S(1)}, u32[]{:S(2)}, u32[]{:S(2)}) %collective-permute-start.8) | collective-permute-done | bytes 786464 | tf_op jit(solution)/shard_map/ppermute | solution.py:341
  109.8 1.5 fusion.46
  111.4 4.0 %collective-permute-start.10 = (bf16[256,512]{1,0:T(8,128)(2,1)S(1)}, bf16[256,512]{1,0:T(8,128)(2,1)S(1)}, u32[]{:S(2)}, u32[]{:S(2)}) collective-permute-start(bf16[256,512]{1,0:T(8,128)(2,1)S(1)} %get-tuple-element.83), channel_id=1, source_target_pairs={{0,8},{8,16},{16,24},{24,32},{32,40},{40,48},{48,56},{56,64},{64,7... | collective-permute-start | bytes 786440 | tf_op jit(solution)/shard_map/ppermute | solution.py:346
  115.4 1.5 collective-permute-start.11
  118.7 4.4 %collective-permute-done.11 = bf16[256,512]{1,0:T(8,128)(2,1)S(1)} collective-permute-done((bf16[256,512]{1,0:T(8,128)(2,1)S(1)}, bf16[256,512]{1,0:T(8,128)(2,1)S(1)}, u32[]{:S(2)}, u32[]{:S(2)}) %collective-permute-start.11) | collective-permute-done | bytes 262176 | tf_op jit(solution)/shard_map/ppermute | solution.py:346
  123.9 40.7 %enc_backward.1 = (bf16[256,512]{1,0:T(8,128)(2,1)}, bf16[1152,512]{1,0:T(8,128)(2,1)}, bf16[512,512]{1,0:T(8,128)(2,1)}, bf16[512,512]{1,0:T(8,128)(2,1)}, bf16[512,512]{1,0:T(8,128)(2,1)}) custom-call(s32[8,1,1024]{2,1,0:T(1,128)} %reshape.159.idx_row_ref, f32[256,32]{1,0:T(8,128)} %get-tuple-element.53.scale_ref, bf16[256,512]{1,0:T(8,128)(2,1)} %bitcast.77, ...), custom_call_target="tpu_custom_call" | custom-call | tf_op jit(solution)/shard_map/enc_backward/pallas_call | solution.py:307
  168.8 5.9 %collective-permute-start.16 = (bf16[1536,512]{1,0:T(8,128)(2,1)}, bf16[1536,512]{1,0:T(8,128)(2,1)}, u32[]{:S(2)}, u32[]{:S(2)}) collective-permute-start(bf16[1536,512]{1,0:T(8,128)(2,1)} %constant_dynamic-slice_fusion), channel_id=1, source_target_pairs={{0,1},{1,0},{2,3},{3,2},{4,5},{5,4},{6,7},{7,6},{8,9},{9,8},{10,11... | collective-permute-start | bytes 4718600 | tf_op jit(solution)/shard_map/ppermute | solution.py:360
  174.7 3.4 %collective-permute-done.16 = bf16[1536,512]{1,0:T(8,128)(2,1)} collective-permute-done((bf16[1536,512]{1,0:T(8,128)(2,1)}, bf16[1536,512]{1,0:T(8,128)(2,1)}, u32[]{:S(2)}, u32[]{:S(2)}) %collective-permute-start.16) | collective-permute-done | bytes 1572896 | tf_op jit(solution)/shard_map/ppermute | solution.py:360
  178.1 1.8 add_convert_fusion
  179.9 39.2 %all_to_all.10 = bf16[64,24,512]{2,1,0:T(8,128)(2,1)S(1)} all-to-all(bf16[64,24,512]{2,1,0:T(8,128)(2,1)S(1)} %bitcast.73), channel_id=1, replica_groups={{0,2,4,6,8,10,12,14,16,18,20,22,24,26,28,30,32,34,36,38,40,42,44,46,48,..., dimensions={0} | all-to-all | bytes 3145728 | tf_op jit(solution)/shard_map/all_to_all | solution.py:362
  220.7 5.9 %all-to-all-start.1 = ((bf16[64,24,512]{2,1,0:T(8,128)(2,1)}), bf16[64,24,512]{2,1,0:T(8,128)(2,1)}, u32[]{:S(2)}, u32[]{:S(2)}) async-start(bf16[64,24,512]{2,1,0:T(8,128)(2,1)} %broadcast_in_dim.4), calls=%async_computation.1 | async-start | bytes 3145728 | tf_op jit(solution)/shard_map/all_to_all | solution.py:365
  226.6 2.2 collective-permute-start.12
  230.3 13.4 %collective-permute-done.12 = bf16[64,512]{1,0:T(8,128)(2,1)S(1)} collective-permute-done((bf16[64,512]{1,0:T(8,128)(2,1)S(1)}, bf16[64,512]{1,0:T(8,128)(2,1)S(1)}, u32[]{:S(2)}, u32[]{:S(2)}) %collective-permute-start.12) | collective-permute-done | bytes 65568 | tf_op jit(solution)/shard_map/ppermute | solution.py:341
  243.9 4.5 %all-to-all-done.1 = bf16[64,24,512]{2,1,0:T(8,128)(2,1)} async-done(((bf16[64,24,512]{2,1,0:T(8,128)(2,1)}), bf16[64,24,512]{2,1,0:T(8,128)(2,1)}, u32[]{:S(2)}, u32[]{:S(2)}) %all-to-all-start.1) | async-done | bytes 1572896 | tf_op jit(solution)/shard_map/all_to_all | solution.py:365
  248.4 3.2 %collective-permute-start.17 = (bf16[1536,512]{1,0:T(8,128)(2,1)}, bf16[1536,512]{1,0:T(8,128)(2,1)}, u32[]{:S(2)}, u32[]{:S(2)}) collective-permute-start(bf16[1536,512]{1,0:T(8,128)(2,1)} %bitcast.19), channel_id=1, source_target_pairs={{0,1},{1,0},{2,3},{3,2},{4,5},{5,4},{6,7},{7,6},{8,9},{9,8},{10,11... | collective-permute-start | bytes 4718600 | tf_op jit(solution)/shard_map/ppermute | solution.py:366
  251.8 2.2 collective-permute-start.14
  255.5 4.3 %collective-permute-done.14 = bf16[256,512]{1,0:T(8,128)(2,1)S(1)} collective-permute-done((bf16[256,512]{1,0:T(8,128)(2,1)S(1)}, bf16[256,512]{1,0:T(8,128)(2,1)S(1)}, u32[]{:S(2)}, u32[]{:S(2)}) %collective-permute-start.14) | collective-permute-done | bytes 262176 | tf_op jit(solution)/shard_map/ppermute | solution.py:346
  259.8 3.8 %collective-permute-done.15 = bf16[256,512]{1,0:T(8,128)(2,1)S(1)} collective-permute-done((bf16[256,512]{1,0:T(8,128)(2,1)S(1)}, bf16[256,512]{1,0:T(8,128)(2,1)S(1)}, u32[]{:S(2)}, u32[]{:S(2)}) %collective-permute-start.15) | collective-permute-done | bytes 262176 | tf_op jit(solution)/shard_map/ppermute | solution.py:346
  265.2 2.3 select_convert_fusion
  267.5 2.7 %fusion.47 = (f32[512,512]{1,0:T(8,128)}, f32[512,512]{1,0:T(8,128)}, f32[512,512]{1,0:T(8,128)}, f32[512,512]{1,0:T(8,128)}, f32[512,512]{1,0:T(8,128)}, /*index=5*/f32[512,512]{1,0:T(8,128)}) fusion(f32[1536,512]{1,0:T(8,128)S(1)} %get-tuple-element.72, f32[1536,512]{1,0:T(8,128)S(1)} %get-tuple-element.73), kind=kLoop, calls=%fused_computation.128 | loop fusion | bytes 12582912 | tf_op jit(solution)/shard_map/slice | solution.py:471
  (91 shorter events, 27.5 us)
Async XLA Ops:
  1.7 9.5 %collective-permute-start = (bf16[256,512]{1,0:T(8,128)(2,1)S(1)}, bf16[256,512]{1,0:T(8,128)(2,1)S(1)}, u32[]{:S(2)}, u32[]{:S(2)}) collective-permute-start(bf16[256,512]{1,0:T(8,128)(2,1)S(1)} %bitcast.81), channel_id=1, source_target_pairs={{8,0},{16,8},{24,16},{32,24},{40,32},{48,40},{56,48},{64,56},{72,6... | collective-permute-start | bytes 786440 | tf_op jit(solution)/shard_map/ppermute | solution.py:346
  3.0 9.0 %collective-permute-start.1 = (bf16[256,512]{1,0:T(8,128)(2,1)S(1)}, bf16[256,512]{1,0:T(8,128)(2,1)S(1)}, u32[]{:S(2)}, u32[]{:S(2)}) collective-permute-start(bf16[256,512]{1,0:T(8,128)(2,1)S(1)} %bitcast.80), channel_id=1, source_target_pairs={{0,8},{8,16},{16,24},{24,32},{32,40},{40,48},{48,56},{56,64},{64,7... | collective-permute-start | bytes 786440 | tf_op jit(solution)/shard_map/ppermute | solution.py:346
  11.2 9.4 %copy-start = (bf16[256,512]{1,0:T(8,128)(2,1)}, bf16[256,512]{1,0:T(8,128)(2,1)S(1)}, u32[]{:S(2)}) copy-start(bf16[256,512]{1,0:T(8,128)(2,1)S(1)} %collective-permute-done.high_ref) | copy-start | bytes 786436
  12.1 8.5 %copy-start.1 = (bf16[256,512]{1,0:T(8,128)(2,1)}, bf16[256,512]{1,0:T(8,128)(2,1)S(1)}, u32[]{:S(2)}) copy-start(bf16[256,512]{1,0:T(8,128)(2,1)S(1)} %collective-permute-done.1.low_ref) | copy-start | bytes 786436
  13.4 4.8 %collective-permute-start.2 = (bf16[64,512]{1,0:T(8,128)(2,1)S(1)}, bf16[64,512]{1,0:T(8,128)(2,1)S(1)}, u32[]{:S(2)}, u32[]{:S(2)}) collective-permute-start(bf16[64,512]{1,0:T(8,128)(2,1)S(1)} %reshape.155), channel_id=1, source_target_pairs={{0,1},{1,2},{2,3},{3,4},{4,5},{5,6},{6,7},{7,0},{8,9},{9,10},{10,1... | collective-permute-start | bytes 196616 | tf_op jit(solution)/shard_map/ppermute | solution.py:341
  16.9 3.7 %collective-permute-start.3 = (bf16[64,512]{1,0:T(8,128)(2,1)S(1)}, bf16[64,512]{1,0:T(8,128)(2,1)S(1)}, u32[]{:S(2)}, u32[]{:S(2)}) collective-permute-start(bf16[64,512]{1,0:T(8,128)(2,1)S(1)} %reshape.156), channel_id=1, source_target_pairs={{0,7},{1,0},{2,1},{3,2},{4,3},{5,4},{6,5},{7,6},{8,15},{9,8},{10,9... | collective-permute-start | bytes 196616 | tf_op jit(solution)/shard_map/ppermute | solution.py:341
  18.2 2.4 copy-start.12
  21.2 42.8 %copy-start.15 = (s32[3,8,64]{2,1,0:T(8,128)S(1)}, s32[3,8,64]{2,1,0:T(8,128)}, u32[]{:S(2)}) copy-start(s32[3,8,64]{2,1,0:T(8,128)} %param.27) | copy-start | bytes 18436
  51.0 11.1 %collective-permute-start.4 = (bf16[256,512]{1,0:T(8,128)(2,1)}, bf16[256,512]{1,0:T(8,128)(2,1)S(1)}, u32[]{:S(2)}, u32[]{:S(2)}) collective-permute-start(bf16[256,512]{1,0:T(8,128)(2,1)} %get-tuple-element.50), channel_id=1, source_target_pairs={{8,0},{16,8},{24,16},{32,24},{40,32},{48,40},{56,48},{64,56},{72,6... | collective-permute-start | bytes 786440 | tf_op jit(solution)/shard_map/ppermute | solution.py:346
  52.3 10.9 %collective-permute-start.5 = (bf16[256,512]{1,0:T(8,128)(2,1)}, bf16[256,512]{1,0:T(8,128)(2,1)S(1)}, u32[]{:S(2)}, u32[]{:S(2)}) collective-permute-start(bf16[256,512]{1,0:T(8,128)(2,1)} %get-tuple-element.50), channel_id=1, source_target_pairs={{0,8},{8,16},{16,24},{24,32},{32,40},{40,48},{48,56},{56,64},{64,7... | collective-permute-start | bytes 786440 | tf_op jit(solution)/shard_map/ppermute | solution.py:346
  63.3 12.1 %copy-start.3 = (bf16[768,512]{1,0:T(8,128)(2,1)}, bf16[768,512]{1,0:T(8,128)(2,1)S(1)}, u32[]{:S(2)}) copy-start(bf16[768,512]{1,0:T(8,128)(2,1)S(1)} %constant_dynamic-update-slice_fusion.centre_ref) | copy-start | bytes 2359300
  63.3 9.3 %collective-permute-start.6 = (bf16[768,512]{1,0:T(8,128)(2,1)S(1)}, bf16[768,512]{1,0:T(8,128)(2,1)S(1)}, u32[]{:S(2)}, u32[]{:S(2)}) collective-permute-start(bf16[768,512]{1,0:T(8,128)(2,1)S(1)} %constant_dynamic-update-slice_fusion.centre_ref), channel_id=1, source_target_pairs={{0,1},{1,2},{2,3},{3,4},{4,5},{5,6},{6,7},{7,0},{8,9},{9,10},{10,1... | collective-permute-start | bytes 2359304 | tf_op jit(solution)/shard_map/ppermute | solution.py:341
  63.7 11.7 %collective-permute-start.7 = (bf16[768,512]{1,0:T(8,128)(2,1)S(1)}, bf16[768,512]{1,0:T(8,128)(2,1)S(1)}, u32[]{:S(2)}, u32[]{:S(2)}) collective-permute-start(bf16[768,512]{1,0:T(8,128)(2,1)S(1)} %constant_dynamic-update-slice_fusion.centre_ref), channel_id=1, source_target_pairs={{0,7},{1,0},{2,1},{3,2},{4,3},{5,4},{6,5},{7,6},{8,15},{9,8},{10,9... | collective-permute-start | bytes 2359304 | tf_op jit(solution)/shard_map/ppermute | solution.py:341
  72.6 2.8 %copy-start.7 = (bf16[768,512]{1,0:T(8,128)(2,1)}, bf16[768,512]{1,0:T(8,128)(2,1)S(1)}, u32[]{:S(2)}) copy-start(bf16[768,512]{1,0:T(8,128)(2,1)S(1)} %collective-permute-done.6.left_ref) | copy-start | bytes 2359300
  97.9 11.9 %collective-permute-start.8 = (bf16[768,512]{1,0:T(8,128)(2,1)}, bf16[768,512]{1,0:T(8,128)(2,1)S(1)}, u32[]{:S(2)}, u32[]{:S(2)}) collective-permute-start(bf16[768,512]{1,0:T(8,128)(2,1)} %get-tuple-element.55), channel_id=1, source_target_pairs={{0,7},{1,0},{2,1},{3,2},{4,3},{5,4},{6,5},{7,6},{8,15},{9,8},{10,9... | collective-permute-start | bytes 2359304 | tf_op jit(solution)/shard_map/ppermute | solution.py:341
  99.3 10.5 %collective-permute-start.9 = (bf16[768,512]{1,0:T(8,128)(2,1)}, bf16[768,512]{1,0:T(8,128)(2,1)S(1)}, u32[]{:S(2)}, u32[]{:S(2)}) collective-permute-start(bf16[768,512]{1,0:T(8,128)(2,1)} %get-tuple-element.56), channel_id=1, source_target_pairs={{0,1},{1,2},{2,3},{3,4},{4,5},{5,6},{6,7},{7,0},{8,9},{9,10},{10,1... | collective-permute-start | bytes 2359304 | tf_op jit(solution)/shard_map/ppermute | solution.py:341
  109.8 7.1 %copy-start.14 = (s32[1,1,256,32]{2,3,1,0:T(8,128)S(1)}, s32[1,1,256,32]{2,3,1,0:T(8,128)}, u32[]{:S(2)}) copy-start(s32[1,1,256,32]{2,3,1,0:T(8,128)} %param.25) | copy-start | bytes 98308
  111.4 7.3 %collective-permute-start.10 = (bf16[256,512]{1,0:T(8,128)(2,1)S(1)}, bf16[256,512]{1,0:T(8,128)(2,1)S(1)}, u32[]{:S(2)}, u32[]{:S(2)}) collective-permute-start(bf16[256,512]{1,0:T(8,128)(2,1)S(1)} %get-tuple-element.83), channel_id=1, source_target_pairs={{0,8},{8,16},{16,24},{24,32},{32,40},{40,48},{48,56},{56,64},{64,7... | collective-permute-start | bytes 786440 | tf_op jit(solution)/shard_map/ppermute | solution.py:346
  115.4 7.7 %collective-permute-start.11 = (bf16[256,512]{1,0:T(8,128)(2,1)S(1)}, bf16[256,512]{1,0:T(8,128)(2,1)S(1)}, u32[]{:S(2)}, u32[]{:S(2)}) collective-permute-start(bf16[256,512]{1,0:T(8,128)(2,1)S(1)} %get-tuple-element.84), channel_id=1, source_target_pairs={{8,0},{16,8},{24,16},{32,24},{40,32},{48,40},{56,48},{64,56},{72,6... | collective-permute-start | bytes 786440 | tf_op jit(solution)/shard_map/ppermute | solution.py:346
  164.6 2.4 copy-start.5
  164.7 2.4 copy-start.16
  164.7 2.8 %copy-start.10 = (bf16[512,512]{1,0:T(8,128)(2,1)S(1)}, bf16[512,512]{1,0:T(8,128)(2,1)}, u32[]{:S(2)}) copy-start(bf16[512,512]{1,0:T(8,128)(2,1)} %get-tuple-element.65) | copy-start | bytes 1572868
  168.8 9.3 %collective-permute-start.16 = (bf16[1536,512]{1,0:T(8,128)(2,1)}, bf16[1536,512]{1,0:T(8,128)(2,1)}, u32[]{:S(2)}, u32[]{:S(2)}) collective-permute-start(bf16[1536,512]{1,0:T(8,128)(2,1)} %constant_dynamic-slice_fusion), channel_id=1, source_target_pairs={{0,1},{1,0},{2,3},{3,2},{4,5},{5,4},{6,7},{7,6},{8,9},{9,8},{10,11... | collective-permute-start | bytes 4718600 | tf_op jit(solution)/shard_map/ppermute | solution.py:360
  219.4 7.2 %copy-start.4 = (bf16[1152,512]{1,0:T(8,128)(2,1)S(1)}, bf16[1152,512]{1,0:T(8,128)(2,1)}, u32[]{:S(2)}) copy-start(bf16[1152,512]{1,0:T(8,128)(2,1)} %get-tuple-element.59) | copy-start | bytes 3538948
  220.7 27.8 %all-to-all-start.1 = ((bf16[64,24,512]{2,1,0:T(8,128)(2,1)}), bf16[64,24,512]{2,1,0:T(8,128)(2,1)}, u32[]{:S(2)}, u32[]{:S(2)}) async-start(bf16[64,24,512]{2,1,0:T(8,128)(2,1)} %broadcast_in_dim.4), calls=%async_computation.1 | async-start | bytes 3145728 | tf_op jit(solution)/shard_map/all_to_all | solution.py:365
  226.6 17.1 %collective-permute-start.12 = (bf16[64,512]{1,0:T(8,128)(2,1)S(1)}, bf16[64,512]{1,0:T(8,128)(2,1)S(1)}, u32[]{:S(2)}, u32[]{:S(2)}) collective-permute-start(bf16[64,512]{1,0:T(8,128)(2,1)S(1)} %get-tuple-element.78), channel_id=1, source_target_pairs={{0,7},{1,0},{2,1},{3,2},{4,3},{5,4},{6,5},{7,6},{8,15},{9,8},{10,9... | collective-permute-start | bytes 196616 | tf_op jit(solution)/shard_map/ppermute | solution.py:341
  228.8 15.0 %collective-permute-start.13 = (bf16[64,512]{1,0:T(8,128)(2,1)S(1)}, bf16[64,512]{1,0:T(8,128)(2,1)S(1)}, u32[]{:S(2)}, u32[]{:S(2)}) collective-permute-start(bf16[64,512]{1,0:T(8,128)(2,1)S(1)} %get-tuple-element.77), channel_id=1, source_target_pairs={{0,1},{1,2},{2,3},{3,4},{4,5},{5,6},{6,7},{7,0},{8,9},{9,10},{10,1... | collective-permute-start | bytes 196616 | tf_op jit(solution)/shard_map/ppermute | solution.py:341
  248.4 16.8 %collective-permute-start.17 = (bf16[1536,512]{1,0:T(8,128)(2,1)}, bf16[1536,512]{1,0:T(8,128)(2,1)}, u32[]{:S(2)}, u32[]{:S(2)}) collective-permute-start(bf16[1536,512]{1,0:T(8,128)(2,1)} %bitcast.19), channel_id=1, source_target_pairs={{0,1},{1,0},{2,3},{3,2},{4,5},{5,4},{6,7},{7,6},{8,9},{9,8},{10,11... | collective-permute-start | bytes 4718600 | tf_op jit(solution)/shard_map/ppermute | solution.py:366
  251.8 7.9 %collective-permute-start.14 = (bf16[256,512]{1,0:T(8,128)(2,1)S(1)}, bf16[256,512]{1,0:T(8,128)(2,1)S(1)}, u32[]{:S(2)}, u32[]{:S(2)}) collective-permute-start(bf16[256,512]{1,0:T(8,128)(2,1)S(1)} %bitcast.83), channel_id=1, source_target_pairs={{0,8},{8,16},{16,24},{24,32},{32,40},{40,48},{48,56},{56,64},{64,7... | collective-permute-start | bytes 786440 | tf_op jit(solution)/shard_map/ppermute | solution.py:346
  254.1 9.5 %collective-permute-start.15 = (bf16[256,512]{1,0:T(8,128)(2,1)S(1)}, bf16[256,512]{1,0:T(8,128)(2,1)S(1)}, u32[]{:S(2)}, u32[]{:S(2)}) collective-permute-start(bf16[256,512]{1,0:T(8,128)(2,1)S(1)} %bitcast.82), channel_id=1, source_target_pairs={{8,0},{16,8},{24,16},{32,24},{40,32},{48,40},{56,48},{64,56},{72,6... | collective-permute-start | bytes 786440 | tf_op jit(solution)/shard_map/ppermute | solution.py:346
  255.4 8.4 %copy-start.2 = (bf16[512,512]{1,0:T(8,128)(2,1)S(1)}, bf16[512,512]{1,0:T(8,128)(2,1)}, u32[]{:S(2)}) copy-start(bf16[512,512]{1,0:T(8,128)(2,1)} %send_ref.1) | copy-start | bytes 1572868
  255.4 8.8 %copy-start.6 = (f32[512,512]{1,0:T(8,128)S(1)}, f32[512,512]{1,0:T(8,128)}, u32[]{:S(2)}) copy-start(f32[512,512]{1,0:T(8,128)} %get-tuple-element.52) | copy-start | bytes 3145732
  (4 other events, 5.5 us)

commit v2 on v1

v2 whole, which is shorter than its diff:
```python
import jax
import jax.numpy as jnp
from jax import lax
from jax.experimental import pallas as pl
from jax.experimental.pallas import tpu as pltpu
from jax.sharding import PartitionSpec as P

REACH = 4
NORM_EPSILON = 1e-05
BF = jnp.bfloat16
F32 = jnp.float32
VMEM_LIMIT = 56 * 1024 * 1024
ENC_TILE = 32
ENC_CHUNK = 4
STRIP = 16
DEC_TILE = 256


def dot(a, b):
    return jnp.dot(a, b, preferred_element_type=F32)


def dot_nt(a, b):
    return lax.dot_general(a, b, (((1,), (1,)), ((), ())), preferred_element_type=F32)


def dot_tn(a, b):
    return lax.dot_general(a, b, (((0,), (0,)), ((), ())), preferred_element_type=F32)


def sigma(v):
    return 0.5 * jnp.tanh(0.5 * v) + 0.5


def normalise(message):
    centred = message - jnp.mean(message, axis=-1, keepdims=True)
    factor = lax.rsqrt(jnp.mean(centred * centred, axis=-1, keepdims=True) + NORM_EPSILON)
    return centred, factor


def one_hot(index, places):
    return jnp.where(index == places, BF(1.0), BF(0.0))


def places_of(shape, dim):
    return lax.broadcasted_iota(jnp.int32, shape, dim).astype(jnp.int16)


def staggered(stages, count):
    for i in range(count + len(stages) - 1):
        for d in range(len(stages) - 1, -1, -1):
            if 0 <= i - d < count:
                stages[d](i - d)


def kernel_params():
    return pltpu.CompilerParams(vmem_limit_bytes=VMEM_LIMIT)


def whole(shape):
    return pl.BlockSpec(shape, lambda t: (0,) * len(shape))


def rows_of(count, width):
    return pl.BlockSpec((count, width), lambda t: (t, 0))


def enc_forward_kernel(
    idx_ref, count_ref, mesh_ref, own_ref, high_ref, low_ref, left_ref, right_ref,
    send_ref, recv_ref, out_ref, dec_send_ref,
    new_ref, moved_ref, before_ref, normed_ref, scale_ref,
    band, onehot, received_all,
):
    step = pl.program_id(0)
    tile, degree = idx_ref.shape
    width = mesh_ref.shape[1]
    band_rows = band.shape[0]
    own = pl.ds(pl.multiple_of(step * tile, tile), tile)

    @pl.when(step == 0)
    def _():
        received_all[...] = dot(mesh_ref[...], recv_ref[...])
        at = 0
        for piece in (own_ref, high_ref, low_ref, left_ref, right_ref):
            count = piece.shape[0]
            band[at : at + count, :] = dot(piece[...], send_ref[...]).astype(BF)
            at += count

    places = places_of((tile, band_rows), 1)
    index = idx_ref[...].astype(jnp.int16)
    received = received_all[own, :]
    lane = lax.broadcasted_iota(jnp.int32, (tile, degree), 1)
    rows = ENC_CHUNK * tile
    state = {"total": jnp.zeros((tile, width), F32), "scales": jnp.zeros((tile, degree), F32)}
    held = {}

    def place(c):
        for k in range(c * ENC_CHUNK, (c + 1) * ENC_CHUNK):
            onehot[k * tile : (k + 1) * tile, :] = one_hot(index[:, k : k + 1], places)

    def gather(c):
        held["gathered", c] = dot(onehot[c * rows : (c + 1) * rows, :], band[...])

    def activate(c):
        before = held.pop(("gathered", c)).reshape(ENC_CHUNK, tile, width) + received[None]
        before_ref[c * rows : (c + 1) * rows, :] = before.reshape(rows, width).astype(BF)
        held["hidden", c] = (before * sigma(before)).reshape(rows, width).astype(BF)

    def project(c):
        held["message", c] = dot(held.pop(("hidden", c)), out_ref[...])

    def norm(c):
        centred, factor = normalise(held.pop(("message", c)))
        normed = (centred * factor).reshape(ENC_CHUNK, tile, width)
        normed_ref[c * rows : (c + 1) * rows, :] = normed.reshape(rows, width).astype(BF)
        factor = factor.reshape(ENC_CHUNK, tile, 1)
        for j in range(ENC_CHUNK):
            k = c * ENC_CHUNK + j
            live = jnp.where(count_ref[...] > k, 1.0, 0.0)
            state["total"] = state["total"] + normed[j] * live
            state["scales"] = jnp.where(lane == k, factor[j] * live, state["scales"])

    staggered([place, gather, activate, project, norm], degree // ENC_CHUNK)
    scale_ref[...] = state["scales"]
    nodes = mesh_ref[own, :].astype(F32)
    new_ref[own, :] = (nodes + degree ** (-0.5) * state["total"]).astype(BF)

    @pl.when(step == pl.num_programs(0) - 1)
    def _():
        moved_ref[...] = dot(new_ref[...], dec_send_ref[...]).astype(BF)


def enc_forward(idx, counts, mesh_rows, pieces, enc_send, enc_recv, enc_out, dec_send):
    nodes, degree = idx.shape
    width = mesh_rows.shape[1]
    tile = ENC_TILE
    edges = tile * degree
    band_rows = sum(p.shape[0] for p in pieces)
    square = whole((width, width))
    return pl.pallas_call(
        enc_forward_kernel,
        name="enc_forward",
        grid=(nodes // tile,),
        in_specs=[rows_of(tile, degree), rows_of(tile, 1), whole((nodes, width))]
        + [whole(p.shape) for p in pieces]
        + [square] * 4,
        out_specs=[
            whole((nodes, width)), whole((nodes, width)),
            rows_of(edges, width), rows_of(edges, width), rows_of(tile, degree),
        ],
        out_shape=[
            jax.ShapeDtypeStruct((nodes, width), BF),
            jax.ShapeDtypeStruct((nodes, width), BF),
            jax.ShapeDtypeStruct((nodes * degree, width), BF),
            jax.ShapeDtypeStruct((nodes * degree, width), BF),
            jax.ShapeDtypeStruct((nodes, degree), F32),
        ],
        scratch_shapes=[
            pltpu.VMEM((band_rows, width), BF),
            pltpu.VMEM((edges, band_rows), BF),
            pltpu.VMEM((nodes, width), F32),
        ],
        compiler_params=kernel_params(),
    )(idx, counts, mesh_rows, *pieces, enc_send, enc_recv, enc_out, dec_send)


def enc_between_kernel(scale_ref, before_ref, normed_ref, out_ref, turned_ref, slope_ref, hidden_ref, sum_ref):
    tile, degree = scale_ref.shape
    width = before_ref.shape[1]
    rows = ENC_CHUNK * tile
    scales = scale_ref[...]
    totals = [jnp.zeros((STRIP, width), F32)] * (tile // STRIP)
    for c in range(degree // ENC_CHUNK):
        part = slice(c * rows, (c + 1) * rows)
        turned = dot_nt(normed_ref[part, :], out_ref[...])
        for k in range(c * ENC_CHUNK, (c + 1) * ENC_CHUNK):
            for i in range(tile // STRIP):
                at = slice(k * tile + i * STRIP, k * tile + (i + 1) * STRIP)
                scale = scales[i * STRIP : (i + 1) * STRIP, k : k + 1]
                before = before_ref[at, :].astype(F32)
                sig = sigma(before)
                silu = before * sig
                slope_ref[at, :] = ((sig + silu * (1.0 - sig)) * scale).astype(BF)
                hidden = silu * scale
                totals[i] = totals[i] + hidden
                hidden_ref[at, :] = hidden.astype(BF)
        turned_ref[part, :] = turned.astype(BF)
    sum_ref[...] = jnp.concatenate(totals, axis=0).astype(BF)


def enc_between(scale, before, normed, enc_out):
    nodes, degree = scale.shape
    width = before.shape[1]
    tile = ENC_TILE
    edges = tile * degree
    per_edge = rows_of(edges, width)
    return pl.pallas_call(
        enc_between_kernel,
        name="enc_between",
        grid=(nodes // tile,),
        in_specs=[rows_of(tile, degree), per_edge, per_edge, whole((width, width))],
        out_specs=[per_edge, per_edge, per_edge, rows_of(tile, width)],
        out_shape=[jax.ShapeDtypeStruct(before.shape, BF)] * 3 + [jax.ShapeDtypeStruct((nodes, width), BF)],
        compiler_params=kernel_params(),
        cost_estimate=pl.CostEstimate(
            flops=2 * before.size * width, bytes_accessed=10 * before.size, transcendentals=before.size
        ),
    )(scale, before, normed, enc_out)


def decoder_kernel(
    idx_ref, idx_row_ref, grid_ref, cot_ref, centre_ref, left_ref, right_ref,
    recv_ref, out_ref,
    new_ref, hidden_ref, message_cot_ref, before_cot_ref, received_cot_ref, left_tot_ref, right_tot_ref,
    onehot, onehot_t, received_all, new_all, received_cot_all,
):
    nodes, width = grid_ref.shape
    degree = idx_ref.shape[1]
    third = centre_ref.shape[0]
    tile = DEC_TILE
    parts = nodes // tile
    index = idx_ref[...].astype(jnp.int16)
    places = places_of((tile, 3 * third), 1)
    held = {}

    received_all[...] = dot(grid_ref[...], recv_ref[...])

    def spot(i):
        h, j = divmod(i, degree)
        return j, slice(h * tile, (h + 1) * tile), slice(i * tile, (i + 1) * tile)

    def place(i):
        j, at, edges = spot(i)
        onehot[edges, :] = one_hot(index[at, j : j + 1], places)

    def gather(i):
        j, at, edges = spot(i)
        gathered = dot(onehot[edges, :third], centre_ref[...])
        gathered = gathered + dot(onehot[edges, third : 2 * third], left_ref[...])
        held["gathered", i] = gathered + dot(onehot[edges, 2 * third :], right_ref[...])

    def activate(i):
        j, at, edges = spot(i)
        before = held.pop(("gathered", i)) + received_all[at, :]
        sig = sigma(before)
        silu = before * sig
        hidden = silu.astype(BF)
        hidden_ref[edges, :] = hidden
        held["slope", i] = sig + silu * (1.0 - sig)
        held["message", i] = dot(hidden, out_ref[...])

    def norm(i):
        j, at, edges = spot(i)
        centred, factor = normalise(held.pop(("message", i)))
        normed = centred * factor
        cot = cot_ref[at, :].astype(F32)
        level = cot - jnp.mean(cot, axis=-1, keepdims=True)
        along = jnp.mean(cot * normed, axis=-1, keepdims=True)
        message_cot = (factor * (level - normed * along)).astype(BF)
        message_cot_ref[edges, :] = message_cot
        held["hidden_cot", i] = dot_nt(message_cot, out_ref[...])
        if j == 0:
            new_all[at, :] = grid_ref[at, :].astype(F32) + normed
        else:
            new_all[at, :] += normed

    def back(i):
        j, at, edges = spot(i)
        before_cot = held.pop(("hidden_cot", i)) * held.pop(("slope", i))
        before_cot_ref[edges, :] = before_cot.astype(BF)
        if j == 0:
            received_cot_all[at, :] = before_cot
        else:
            received_cot_all[at, :] += before_cot
        rows = lax.broadcasted_iota(jnp.int32, (2 * third, tile), 0) + third
        picks = jnp.broadcast_to(idx_row_ref[j : j + 1, at], (16, tile)).astype(jnp.int16)[:1]
        onehot_t[:, edges] = one_hot(picks, rows.astype(jnp.int16))

    staggered([place, gather, activate, norm, back], degree * parts)
    left_tot_ref[...] = dot(onehot_t[:third, :], before_cot_ref[...]).astype(BF)
    new_ref[...] = new_all[...].astype(BF)
    right_tot_ref[...] = dot(onehot_t[third:, :], before_cot_ref[...]).astype(BF)
    received_cot_ref[...] = received_cot_all[...].astype(BF)


def decoder(idx, idx_rows, grid_rows, cot_rows, centre, left, right, dec_recv, dec_out):
    nodes, width = grid_rows.shape
    degree = idx.shape[1]
    third = centre.shape[0]
    edge_shape = jax.ShapeDtypeStruct((degree * nodes, width), BF)
    node_shape = jax.ShapeDtypeStruct((nodes, width), BF)
    side_shape = jax.ShapeDtypeStruct((third, width), BF)
    return pl.pallas_call(
        decoder_kernel,
        name="decoder",
        out_shape=[node_shape, edge_shape, edge_shape, edge_shape, node_shape, side_shape, side_shape],
        scratch_shapes=[
            pltpu.VMEM((degree * nodes, 3 * third), BF),
            pltpu.VMEM((2 * third, degree * nodes), BF),
            pltpu.VMEM((nodes, width), F32),
            pltpu.VMEM((nodes, width), F32),
            pltpu.VMEM((nodes, width), F32),
        ],
        compiler_params=kernel_params(),
    )(idx, idx_rows, grid_rows, cot_rows, centre, left, right, dec_recv, dec_out)


def decoder_rest_kernel(
    idx_row_ref, grid_ref, cot_ref, hidden_ref, message_cot_ref, before_cot_ref, received_cot_ref, recv_ref,
    part_ref, out_grad_ref, recv_grad_ref, centre_tot_ref,
    onehot_t,
):
    third, width = centre_tot_ref.shape
    degree, nodes = idx_row_ref.shape
    tile = DEC_TILE
    rows = places_of((third, tile), 0)
    for i in range(degree * nodes // tile):
        h, j = divmod(i, degree)
        picks = jnp.broadcast_to(idx_row_ref[j : j + 1, h * tile : (h + 1) * tile], (16, tile))
        onehot_t[:, i * tile : (i + 1) * tile] = one_hot(picks.astype(jnp.int16)[:1], rows)
    centre_tot_ref[...] = dot(onehot_t[...], before_cot_ref[...]).astype(BF)
    out_grad_ref[...] = dot_tn(hidden_ref[...], message_cot_ref[...]).astype(BF)
    received_cot = received_cot_ref[...]
    recv_grad_ref[...] = dot_tn(grid_ref[...], received_cot).astype(BF)
    part_ref[...] = cot_ref[...].astype(F32) + dot_nt(received_cot, recv_ref[...])


def decoder_rest(idx_rows, grid_rows, cot_rows, hidden, message_cot, before_cot, received_cot, dec_recv, third):
    degree, nodes = idx_rows.shape
    width = hidden.shape[1]
    return pl.pallas_call(
        decoder_rest_kernel,
        name="decoder_rest",
        out_shape=[
            jax.ShapeDtypeStruct((nodes, width), F32),
            jax.ShapeDtypeStruct((width, width), BF),
            jax.ShapeDtypeStruct((width, width), BF),
            jax.ShapeDtypeStruct((third, width), BF),
        ],
        scratch_shapes=[pltpu.VMEM((third, degree * nodes), BF)],
        compiler_params=kernel_params(),
        cost_estimate=pl.CostEstimate(
            flops=2 * degree * nodes * width * (third + 2 * width), bytes_accessed=8 * degree * nodes * width,
            transcendentals=0,
        ),
    )(idx_rows, grid_rows, cot_rows, hidden, message_cot, before_cot, received_cot, dec_recv)


def enc_backward_kernel(
    idx_row_ref, mesh_ref, moved_cot_ref, sum_ref, normed_ref, turned_ref, slope_ref, hidden_ref,
    own_ref, high_ref, low_ref, left_ref, right_ref,
    dec_send_ref, recv_ref, out_ref,
    mesh_grad_ref, band_cot_ref, grads_ref,
    onehot_t0, onehot_t1, cot0, cot1, weighted, totals, out_acc, node_cot, turned_level, received_cot,
):
    step = pl.program_id(0)
    nodes, width = mesh_ref.shape
    edges = normed_ref.shape[0]
    band_rows = totals.shape[0]
    tiles = pl.num_programs(0) - 1
    tile = ENC_TILE
    degree = edges // tile
    scaling = degree ** (-0.5)
    cots = (cot0, cot1)
    onehots = (onehot_t0, onehot_t1)

    @pl.when(step == 0)
    def _():
        totals[...] = jnp.zeros_like(totals)
        cot = dot_nt(moved_cot_ref[...], dec_send_ref[...])
        node_cot[...] = cot
        spread = scaling * cot
        level = (spread - jnp.mean(spread, axis=-1, keepdims=True)).astype(BF)
        turned_level[...] = dot_nt(level, out_ref[...])
        out_acc[...] = dot_tn(sum_ref[...], level)

    def scatter(slot, n):
        half = width // 2
        at = slice(n * half, (n + 1) * half)
        totals[:, at] += dot(onehots[slot][...], cots[slot][:, at])

    def edge_part(slot, beside):
        strips = tile // STRIP
        total = [jnp.zeros((STRIP, width), F32)] * strips
        for n in range(2):
            if beside is not None:
                scatter(beside, n)
            for k in range(n * degree // 2, (n + 1) * degree // 2):
                for i in range(strips):
                    at = slice(k * tile + i * STRIP, k * tile + (i + 1) * STRIP)
                    mine = pl.ds(pl.multiple_of(step * tile + i * STRIP, STRIP), STRIP)
                    spread = scaling * node_cot[mine, :]
                    along = jnp.mean(spread * normed_ref[at, :].astype(F32), axis=-1, keepdims=True)
                    turned = turned_level[mine, :] - along * turned_ref[at, :].astype(F32)
                    before_cot = slope_ref[at, :].astype(F32) * turned
                    total[i] = total[i] + before_cot
                    cots[slot][at, :] = before_cot.astype(BF)
                    weighted[at, :] = (hidden_ref[at, :].astype(F32) * (-along)).astype(BF)
            part = slice(n * edges // 2, (n + 1) * edges // 2)
            out_acc[...] += dot_tn(weighted[part, :], normed_ref[part, :])
        places = places_of((band_rows, edges), 0)
        spot = jnp.broadcast_to(idx_row_ref[0], (16, edges)).astype(jnp.int16)[:1]
        onehots[slot][...] = one_hot(spot, places)
        received_cot[pl.ds(pl.multiple_of(step * tile, tile), tile), :] = jnp.concatenate(total, axis=0).astype(BF)

    @pl.when(step == 0)
    def _():
        edge_part(0, None)

    for parity in range(2):
        @pl.when((step > 0) & (step < tiles) & (step % 2 == parity))
        def _():
            edge_part(parity, 1 - parity)

    @pl.when(step == tiles)
    def _():
        scatter(1, 0)
        scatter(1, 1)
        grads_ref[width : 2 * width, :] = dot_tn(mesh_ref[...], received_cot[...]).astype(BF)
        grads_ref[2 * width :, :] = out_acc[...].astype(BF)
        mesh_grad_ref[...] = (node_cot[...] + dot_nt(received_cot[...], recv_ref[...])).astype(BF)
        band_cot_ref[...] = totals[...].astype(BF)
        at = 0
        send_grad = jnp.zeros((width, width), F32)
        for piece in (own_ref, high_ref, low_ref, left_ref, right_ref):
            count = piece.shape[0]
            send_grad = send_grad + dot_tn(piece[...], band_cot_ref[at : at + count, :])
            at += count
        grads_ref[:width, :] = send_grad.astype(BF)


def enc_backward(idx_rows, mesh_rows, moved_cot, sums, normed, turned, slope, hidden, pieces, dec_send, enc_recv, enc_out):
    nodes, width = mesh_rows.shape
    tile = ENC_TILE
    tiles = nodes // tile
    assert tiles % 2 == 0
    edges = normed.shape[0] // tiles
    band_rows = sum(p.shape[0] for p in pieces)
    square = whole((width, width))
    last = tiles - 1
    per_node = whole((nodes, width))
    per_edge = pl.BlockSpec((edges, width), lambda t: (jnp.minimum(t, last), 0))
    return pl.pallas_call(
        enc_backward_kernel,
        name="enc_backward",
        grid=(tiles + 1,),
        in_specs=[pl.BlockSpec((1, 1, edges), lambda t: (jnp.minimum(t, last), 0, 0))]
        + [per_node] * 3
        + [per_edge] * 4
        + [whole(p.shape) for p in pieces]
        + [square] * 3,
        out_specs=[per_node, whole((band_rows, width)), whole((3 * width, width))],
        out_shape=[
            jax.ShapeDtypeStruct((nodes, width), BF),
            jax.ShapeDtypeStruct((band_rows, width), BF),
            jax.ShapeDtypeStruct((3 * width, width), BF),
        ],
        scratch_shapes=[
            pltpu.VMEM((band_rows, edges), BF),
            pltpu.VMEM((band_rows, edges), BF),
            pltpu.VMEM((edges, width), BF),
            pltpu.VMEM((edges, width), BF),
            pltpu.VMEM((edges, width), BF),
            pltpu.VMEM((band_rows, width), F32),
            pltpu.VMEM((width, width), F32),
            pltpu.VMEM((nodes, width), F32),
            pltpu.VMEM((nodes, width), F32),
            pltpu.VMEM((nodes, width), BF),
        ],
        compiler_params=kernel_params(),
    )(idx_rows, mesh_rows, moved_cot, sums, normed, turned, slope, hidden, *pieces, dec_send, enc_recv, enc_out)


def to_lon(shard, by):
    count = lax.axis_size("lon")
    return lax.ppermute(shard, "lon", [(i, (i + by) % count) for i in range(count)])


def to_lat(shard, by):
    count = lax.axis_size("lat")
    return lax.ppermute(shard, "lat", [(i, i + by) for i in range(count) if 0 <= i + by < count])


def summed_everywhere(first, second):
    axes = ("lat", "lon")
    lon_count = lax.axis_size("lon")
    count = lax.axis_size("lat") * lon_count
    rows, width = first.shape
    leads = lax.axis_index("lon") % 2 == 0
    swap = [(i, i ^ 1) for i in range(lon_count)]
    alike = [[i for i in range(count) if i % 2 == c] for c in range(2)]
    given = jnp.where(leads, second, first)
    kept = jnp.where(leads, first, second).astype(F32) + lax.ppermute(given, "lon", swap).astype(F32)
    parts = kept.astype(BF).reshape(count // 2, 2 * rows // count, width)
    got = lax.all_to_all(parts, axes, 0, 0, axis_index_groups=alike, tiled=True)
    mine = jnp.sum(got.astype(F32), axis=0).astype(BF)
    spread = jnp.broadcast_to(mine[None], parts.shape)
    ours = lax.all_to_all(spread, axes, 0, 0, axis_index_groups=alike, tiled=True).reshape(rows, width)
    theirs = lax.ppermute(ours, "lon", swap)
    return jnp.where(leads, ours, theirs).astype(F32), jnp.where(leads, theirs, ours).astype(F32)


def on_device(
    grid, mesh_nodes, grid_cot, enc_send, enc_recv, enc_out, dec_send, dec_recv, dec_out,
    enc_src, enc_live, dec_src,
):
    lat_cells, lon_cells, width = grid.shape
    slots, degree = enc_src.shape[2:]
    lat_index = lax.axis_index("lat")
    lon_index = lax.axis_index("lon")
    lon_count = lax.axis_size("lon")
    lon_total = lon_cells * lon_count
    cells = lat_cells * lon_cells
    edge_rows = REACH * lon_cells
    tall = lat_cells + 2 * REACH

    grid_rows = grid.reshape(cells, width)
    mesh_rows = mesh_nodes.reshape(slots, width)
    high = to_lat(grid_rows[:edge_rows], -1)
    low = to_lat(grid_rows[cells - edge_rows :], 1)
    inner = jnp.concatenate([grid_rows, high, low], axis=0).reshape(tall, lon_cells, width)
    left = to_lon(inner[:, lon_cells - REACH :].reshape(tall * REACH, width), 1)
    right = to_lon(inner[:, :REACH].reshape(tall * REACH, width), -1)
    pieces = (grid_rows, high, low, left, right)

    source = enc_src.reshape(slots, degree)
    row = (source // lon_total - lat_index * lat_cells) % tall
    col = (source % lon_total - lon_index * lon_cells + REACH) % lon_total - REACH
    inner_rows = tall * lon_cells
    enc_idx = jnp.where(
        col < 0,
        inner_rows + row * REACH + col + REACH,
        jnp.where(
            col >= lon_cells,
            inner_rows + tall * REACH + row * REACH + col - lon_cells,
            row * lon_cells + col,
        ),
    )
    tiles = slots // ENC_TILE
    enc_idx_rows = enc_idx.reshape(tiles, ENC_TILE, degree).transpose(0, 2, 1)
    enc_idx_rows = enc_idx_rows.reshape(tiles, 1, ENC_TILE * degree)
    counts = jnp.sum(enc_live.reshape(slots, degree), axis=1, keepdims=True)

    picks = dec_src.reshape(3, cells)
    owner = picks // slots
    owner_lat = (owner // lon_count - lat_index) % 3
    owner_lon = (owner % lon_count - lon_index + lon_count) % lon_count
    owner_lon = jnp.where(owner_lon == lon_count - 1, 1, owner_lon * 2)
    dec_idx_rows = (owner_lon * 3 + owner_lat) * slots + picks % slots

    mesh_new, moved, before, normed, scale = enc_forward(
        enc_idx, counts, mesh_rows, pieces, enc_send, enc_recv, enc_out, dec_send
    )

    above = to_lat(moved, -1)
    below = to_lat(moved, 1)
    turned, slope, hidden, sums = enc_between(scale, before, normed, enc_out)
    centre = jnp.concatenate([moved, above, below], axis=0)
    west = to_lon(centre, 1)
    east = to_lon(centre, -1)
    cot_rows = grid_cot.reshape(cells, width)
    grid_new, dec_hidden, dec_message_cot, dec_before_cot, dec_received_cot, west_tot, east_tot = decoder(
        dec_idx_rows.T, dec_idx_rows, grid_rows, cot_rows, centre, west, east, dec_recv, dec_out
    )
    from_east = to_lon(west_tot, -1)
    from_west = to_lon(east_tot, 1)
    grid_part, dec_out_grad, dec_recv_grad, centre_tot = decoder_rest(
        dec_idx_rows, grid_rows, cot_rows, dec_hidden, dec_message_cot, dec_before_cot, dec_received_cot,
        dec_recv, 3 * slots,
    )
    column = centre_tot.astype(F32) + from_east.astype(F32) + from_west.astype(F32)
    from_below = to_lat(column[slots : 2 * slots].astype(BF), 1)
    from_above = to_lat(column[2 * slots :].astype(BF), -1)
    moved_cot = column[:slots] + from_below.astype(F32) + from_above.astype(F32)
    moved_cot = moved_cot.astype(BF)
    dec_send_grad = dot_tn(mesh_new, moved_cot).astype(BF)

    mesh_grad, band_cot, enc_stack = enc_backward(
        enc_idx_rows, mesh_rows, moved_cot, sums, normed, turned, slope, hidden, pieces, dec_send, enc_recv, enc_out
    )
    dec_stack = jnp.concatenate([dec_send_grad, dec_recv_grad, dec_out_grad], axis=0)
    enc_grads, dec_grads = summed_everywhere(enc_stack, dec_stack)

    side = tall * REACH
    from_right = to_lon(band_cot[inner_rows : inner_rows + side], -1)
    from_left = to_lon(band_cot[inner_rows + side :], 1)
    inner_cot = band_cot[:inner_rows].astype(F32).reshape(tall, lon_cells, width)
    inner_cot = inner_cot.at[:, lon_cells - REACH :].add(from_right.astype(F32).reshape(tall, REACH, width))
    inner_cot = inner_cot.at[:, :REACH].add(from_left.astype(F32).reshape(tall, REACH, width))
    inner_cot = inner_cot.reshape(inner_rows, width)
    from_low = to_lat(inner_cot[cells : cells + edge_rows].astype(BF), 1)
    from_high = to_lat(inner_cot[cells + edge_rows :].astype(BF), -1)
    sent_cot = inner_cot[:cells] + jnp.concatenate([from_low, from_high], axis=0).astype(F32)
    grid_grad = (grid_part + dot_nt(sent_cot.astype(BF), enc_send)).astype(BF)

    return (
        grid_new.reshape(grid.shape),
        grid_grad.reshape(grid.shape),
        mesh_grad.reshape(mesh_nodes.shape),
        enc_grads[:width],
        enc_grads[width : 2 * width],
        enc_grads[2 * width :],
        dec_grads[:width],
        dec_grads[width : 2 * width],
        dec_grads[2 * width :],
    )


def solution(mesh):
    node = P("lat", "lon", None)
    block = P("lat", "lon", None, None)
    placed = (
        node, block, node, P(), P(), P(), P(), P(), P(), block, block, P(None, "lat", "lon"),
    )
    return jax.shard_map(
        on_device,
        mesh=mesh,
        in_specs=placed,
        out_specs=(node, node, block, P(), P(), P(), P(), P(), P()),
        check_vma=False,
    )
```

time: 272 us -> 261 us (0.960)
  waiting for transfers between devices: 64.4 us -> 51.9 us
  Pallas kernels: 92.1 us -> 99.8 us
    pallas_call x2 -> x4, Pallas kernels: 62.3 us -> 73.7 us  [the longest x1 31.6 us: enc_backward(): pl.pallas_call(enc_backward_kernel, name='enc_backward', grid=(tiles + 1,...]
    ppermute x8, waiting for transfers between devices: 36.1 us -> 25.2 us  [to_lon(): lax.ppermute(shard, 'lon', [(i, (i + by) % count) for i in range(count)])]
    pallas_call x1, Pallas kernels: 29.8 us -> 26.1 us  [enc_forward(): pl.pallas_call(enc_forward_kernel, name='enc_forward', grid=(nodes // til...]
    ppermute x8, waiting for transfers between devices: 20.4 us -> 16.7 us  [to_lat(): lax.ppermute(shard, 'lat', [(i, i + by) for i in range(count) if 0 <= i +...]
    unnamed x42 -> x41, local copies, waits for them, and re-layouts: 6.69 us -> 4.51 us
  transfers between devices with their start and end apart: 19 -> 19, of which waited for: 16 -> 13; matrix products, arithmetic and copies ran while one was open for 4% -> 3% of each run, Pallas kernels for 0% -> 11%
where the time goes in v2:
time: 261 us; the launch traced here: 259 us
  Pallas kernels  99.8 us (38%)
  waiting for transfers between devices  51.9 us (20%)
  starting transfers between devices  43.3 us (17%)
  blocking collectives  39.2 us (15%)
  local copies, waits for them, and re-layouts  12.6 us (5%)
  other arithmetic  9.94 us (4%)
    all_to_all x1, blocking collectives, summed_everywhere(): got = lax.all_to_all(parts, axes, 0, 0, axis_index_groups=alike, tiled=True)  39.2 us
    pallas_call x1, Pallas kernels, enc_backward(): pl.pallas_call(enc_backward_kernel, name='enc_backward', grid=(tiles + 1,...  31.6 us
    pallas_call x1, Pallas kernels, enc_forward(): pl.pallas_call(enc_forward_kernel, name='enc_forward', grid=(nodes // til...  26.1 us
    ppermute x8, waiting for transfers between devices, to_lon(): lax.ppermute(shard, 'lon', [(i, (i + by) % count) for i in range(count)])  25.2 us
    pallas_call x1, Pallas kernels, enc_between(): pl.pallas_call(enc_between_kernel, name='enc_between', grid=(nodes // til...  22.7 us
    ppermute x8, starting transfers between devices, to_lat(): lax.ppermute(shard, 'lat', [(i, i + by) for i in range(count) if 0 <= i +...  20.9 us
    ppermute x8, waiting for transfers between devices, to_lat(): lax.ppermute(shard, 'lat', [(i, i + by) for i in range(count) if 0 <= i +...  16.7 us
    pallas_call x1, Pallas kernels, decoder(): pl.pallas_call(decoder_kernel, name='decoder', out_shape=[node_shape, edg...  12.7 us
  transfers between devices with their start and end apart: 19, of which 13 were waited for; matrix products, arithmetic and copies ran while one was open for 3% of the time, Pallas kernels for 11%

profile of v2, /device:TPU:1, one launch (start us, length us, event | category | flops | bytes accessed | tf_op | source)
XLA Modules:
  0.0 258.6 jit_solution(12784767399205548388)
XLA Ops:
  3.1 4.6 %collective-permute-start.1 = (bf16[256,512]{1,0:T(8,128)(2,1)S(1)}, bf16[256,512]{1,0:T(8,128)(2,1)S(1)}, u32[]{:S(2)}, u32[]{:S(2)}) collective-permute-start(bf16[256,512]{1,0:T(8,128)(2,1)S(1)} %bitcast.65), channel_id=1, source_target_pairs={{0,8},{8,16},{16,24},{24,32},{32,40},{40,48},{48,56},{56,64},{64,7... | collective-permute-start | bytes 786440 | tf_op jit(solution)/shard_map/ppermute | solution.py:481
  8.6 2.7 %collective-permute-done.high_ref = bf16[256,512]{1,0:T(8,128)(2,1)S(1)} collective-permute-done((bf16[256,512]{1,0:T(8,128)(2,1)S(1)}, bf16[256,512]{1,0:T(8,128)(2,1)S(1)}, u32[]{:S(2)}, u32[]{:S(2)}) %collective-permute-start) | collective-permute-done | bytes 262176 | tf_op jit(solution)/shard_map/ppermute | solution.py:481
  12.3 3.5 %collective-permute-start.2 = (bf16[64,512]{1,0:T(8,128)(2,1)S(1)}, bf16[64,512]{1,0:T(8,128)(2,1)S(1)}, u32[]{:S(2)}, u32[]{:S(2)}) collective-permute-start(bf16[64,512]{1,0:T(8,128)(2,1)S(1)} %reshape.154), channel_id=1, source_target_pairs={{0,1},{1,2},{2,3},{3,4},{4,5},{5,6},{6,7},{7,0},{8,9},{9,10},{10,1... | collective-permute-start | bytes 196616 | tf_op jit(solution)/shard_map/ppermute | solution.py:476
  17.6 1.9 collective-permute-done.3.right_ref
  20.1 26.1 %enc_forward.1 = (bf16[256,512]{1,0:T(8,128)(2,1)}, bf16[256,512]{1,0:T(8,128)(2,1)}, bf16[8192,512]{1,0:T(8,128)(2,1)}, bf16[8192,512]{1,0:T(8,128)(2,1)}, f32[256,32]{1,0:T(8,128)}) custom-call(s32[256,32]{1,0:T(8,128)} %select_select_fusion.idx_ref, s32[256,1]{1,0:T(8,128)} %copy.28.count_ref, bf16[256,512]{1,0:T(8,128)(2,1)} %bitcast.60, ...), custom_call_target="tpu_custom_call" | custom-call | tf_op jit(solution)/shard_map/enc_forward/pallas_call | solution.py:140
  47.5 4.9 %collective-permute-start.5 = (bf16[256,512]{1,0:T(8,128)(2,1)}, bf16[256,512]{1,0:T(8,128)(2,1)S(1)}, u32[]{:S(2)}, u32[]{:S(2)}) collective-permute-start(bf16[256,512]{1,0:T(8,128)(2,1)} %get-tuple-element.56), channel_id=1, source_target_pairs={{0,8},{8,16},{16,24},{24,32},{32,40},{40,48},{48,56},{56,64},{64,7... | collective-permute-start | bytes 786440 | tf_op jit(solution)/shard_map/ppermute | solution.py:481
  53.4 3.9 %collective-permute-done.4 = bf16[256,512]{1,0:T(8,128)(2,1)S(1)} collective-permute-done((bf16[256,512]{1,0:T(8,128)(2,1)}, bf16[256,512]{1,0:T(8,128)(2,1)S(1)}, u32[]{:S(2)}, u32[]{:S(2)}) %collective-permute-start.4) | collective-permute-done | bytes 262176 | tf_op jit(solution)/shard_map/ppermute | solution.py:481
  60.8 7.0 %collective-permute-done.6.left_ref = bf16[768,512]{1,0:T(8,128)(2,1)S(1)} collective-permute-done((bf16[768,512]{1,0:T(8,128)(2,1)S(1)}, bf16[768,512]{1,0:T(8,128)(2,1)S(1)}, u32[]{:S(2)}, u32[]{:S(2)}) %collective-permute-start.6) | collective-permute-done | bytes 786464 | tf_op jit(solution)/shard_map/ppermute | solution.py:476
  67.9 2.8 %collective-permute-done.7.right_ref = bf16[768,512]{1,0:T(8,128)(2,1)S(1)} collective-permute-done((bf16[768,512]{1,0:T(8,128)(2,1)S(1)}, bf16[768,512]{1,0:T(8,128)(2,1)S(1)}, u32[]{:S(2)}, u32[]{:S(2)}) %collective-permute-start.7) | collective-permute-done | bytes 786464 | tf_op jit(solution)/shard_map/ppermute | solution.py:476
  71.5 12.7 %decoder.1 = (bf16[512,512]{1,0:T(8,128)(2,1)}, bf16[1536,512]{1,0:T(8,128)(2,1)}, bf16[1536,512]{1,0:T(8,128)(2,1)}, bf16[1536,512]{1,0:T(8,128)(2,1)}, bf16[51...) custom-call(s32[512,3]{1,0:T(8,128)} %copy.29.idx_ref, s32[3,512]{1,0:T(4,128)} %fusion.29.idx_row_ref, ...), custom_call_target="tpu_custom_call" | custom-call | tf_op jit(solution)/shard_map/decoder/pallas_call | solution.py:293
  84.2 1.4 collective-permute-start.8
  87.1 6.7 %decoder_rest.1 = (f32[512,512]{1,0:T(8,128)}, bf16[512,512]{1,0:T(8,128)(2,1)}, bf16[512,512]{1,0:T(8,128)(2,1)}, bf16[768,512]{1,0:T(8,128)(2,1)}) custom-call(s32[3,512]{1,0:T(4,128)} %fusion.29.idx_row_ref, bf16[512,512]{1,0:T(8,128)(2,1)} %bitcast.54, bf16[512,512]{1,0:T(8,128)(2,1)} %bitcast.63, bf16[1536,512]{1,0:T(8,128)(2,1)} %get-tuple-element.58.hidden_ref, ...), custom_call_target="tpu_custom_call" | custom-call | flops 2818572288 | bytes 6291456 | tf_op jit(solution)/shard_map/decoder_rest/pallas_call | solution.py:331
  93.8 2.3 collective-permute-done.8
  96.1 1.5 fusion.33
  97.7 4.0 %collective-permute-start.10 = (bf16[256,512]{1,0:T(8,128)(2,1)S(1)}, bf16[256,512]{1,0:T(8,128)(2,1)S(1)}, u32[]{:S(2)}, u32[]{:S(2)}) collective-permute-start(bf16[256,512]{1,0:T(8,128)(2,1)S(1)} %get-tuple-element.95), channel_id=1, source_target_pairs={{0,8},{8,16},{16,24},{24,32},{32,40},{40,48},{48,56},{56,64},{64,7... | collective-permute-start | bytes 786440 | tf_op jit(solution)/shard_map/ppermute | solution.py:481
  103.0 22.7 %enc_between.1 = (bf16[8192,512]{1,0:T(8,128)(2,1)}, bf16[8192,512]{1,0:T(8,128)(2,1)}, bf16[8192,512]{1,0:T(8,128)(2,1)}, bf16[256,512]{1,0:T(8,128)(2,1)}) custom-call(f32[256,32]{1,0:T(8,128)} %get-tuple-element.66.scale_ref, bf16[8192,512]{1,0:T(8,128)(2,1)} %get-tuple-element.67.before_ref, bf16[8192,512]{1,0:T(8,128)(2,1)} %get-tuple-element.68.normed_ref, ...), custom_call_target="tpu_custom_call" | custom-call | flops 4294967296 | bytes 41943040 | tf_op jit(solution)/shard_map/enc_between/pallas_call | solution.py:197
  126.6 31.6 %enc_backward.1 = (bf16[256,512]{1,0:T(8,128)(2,1)}, bf16[1152,512]{1,0:T(8,128)(2,1)}, bf16[1536,512]{1,0:T(8,128)(2,1)}) custom-call(s32[8,1,1024]{2,1,0:T(1,128)} %reshape.158.idx_row_ref, bf16[256,512]{1,0:T(8,128)(2,1)} %bitcast.61, bf16[256,512]{1,0:T(8,128)(2,1)} %copy-done.2, bf16[256,512]{1,0:T(8,128)(2,1)} %get-tuple-element.69.sum_ref, ...), custom_call_target="tpu_custom_call" | custom-call | tf_op jit(solution)/shard_map/enc_backward/pallas_call | solution.py:443
  158.2 2.0 broadcast_select_fusion
  160.2 4.1 %collective-permute-start.16 = (bf16[1536,512]{1,0:T(8,128)(2,1)S(1)}, bf16[1536,512]{1,0:T(8,128)(2,1)S(1)}, u32[]{:S(2)}, u32[]{:S(2)}) collective-permute-start(bf16[1536,512]{1,0:T(8,128)(2,1)S(1)} %broadcast_select_fusion), channel_id=1, source_target_pairs={{0,1},{1,0},{2,3},{3,2},{4,5},{5,4},{6,7},{7,6},{8,9},{9,8},{10,11... | collective-permute-start | bytes 4718600 | tf_op jit(solution)/shard_map/ppermute | solution.py:493
  164.3 3.0 %collective-permute-done.16 = bf16[1536,512]{1,0:T(8,128)(2,1)S(1)} collective-permute-done((bf16[1536,512]{1,0:T(8,128)(2,1)S(1)}, bf16[1536,512]{1,0:T(8,128)(2,1)S(1)}, u32[]{:S(2)}, u32[]{:S(2)}) %collective-permute-start.16) | collective-permute-done | bytes 1572896 | tf_op jit(solution)/shard_map/ppermute | solution.py:493
  167.9 39.2 %all_to_all.10 = bf16[64,24,512]{2,1,0:T(8,128)(2,1)S(1)} all-to-all(bf16[64,24,512]{2,1,0:T(8,128)(2,1)S(1)} %bitcast.57), channel_id=1, replica_groups={{0,2,4,6,8,10,12,14,16,18,20,22,24,26,28,30,32,34,36,38,40,42,44,46,48,..., dimensions={0} | all-to-all | bytes 3145728 | tf_op jit(solution)/shard_map/all_to_all | solution.py:495
  208.7 6.0 %all-to-all-start.1 = ((bf16[64,24,512]{2,1,0:T(8,128)(2,1)}), bf16[64,24,512]{2,1,0:T(8,128)(2,1)}, u32[]{:S(2)}, u32[]{:S(2)}) async-start(bf16[64,24,512]{2,1,0:T(8,128)(2,1)} %broadcast_in_dim.12), calls=%async_computation.1 | async-start | bytes 3145728 | tf_op jit(solution)/shard_map/all_to_all | solution.py:498
  214.7 2.0 collective-permute-start.12
  218.2 11.1 %collective-permute-done.12 = bf16[64,512]{1,0:T(8,128)(2,1)S(1)} collective-permute-done((bf16[64,512]{1,0:T(8,128)(2,1)S(1)}, bf16[64,512]{1,0:T(8,128)(2,1)S(1)}, u32[]{:S(2)}, u32[]{:S(2)}) %collective-permute-start.12) | collective-permute-done | bytes 65568 | tf_op jit(solution)/shard_map/ppermute | solution.py:476
  229.5 6.9 %all-to-all-done.1 = bf16[64,24,512]{2,1,0:T(8,128)(2,1)} async-done(((bf16[64,24,512]{2,1,0:T(8,128)(2,1)}), bf16[64,24,512]{2,1,0:T(8,128)(2,1)}, u32[]{:S(2)}, u32[]{:S(2)}) %all-to-all-start.1) | async-done | bytes 1572896 | tf_op jit(solution)/shard_map/all_to_all | solution.py:498
  236.4 3.2 %collective-permute-start.17 = (bf16[1536,512]{1,0:T(8,128)(2,1)}, bf16[1536,512]{1,0:T(8,128)(2,1)S(1)}, u32[]{:S(2)}, u32[]{:S(2)}) collective-permute-start(bf16[1536,512]{1,0:T(8,128)(2,1)} %bitcast.19), channel_id=1, source_target_pairs={{0,1},{1,0},{2,3},{3,2},{4,5},{5,4},{6,7},{7,6},{8,9},{9,8},{10,11... | collective-permute-start | bytes 4718600 | tf_op jit(solution)/shard_map/ppermute | solution.py:499
  239.9 2.2 collective-permute-start.14
  242.2 1.3 collective-permute-start.15
  243.6 4.3 %collective-permute-done.14 = bf16[256,512]{1,0:T(8,128)(2,1)S(1)} collective-permute-done((bf16[256,512]{1,0:T(8,128)(2,1)S(1)}, bf16[256,512]{1,0:T(8,128)(2,1)S(1)}, u32[]{:S(2)}, u32[]{:S(2)}) %collective-permute-start.14) | collective-permute-done | bytes 262176 | tf_op jit(solution)/shard_map/ppermute | solution.py:481
  247.9 3.8 %collective-permute-done.15 = bf16[256,512]{1,0:T(8,128)(2,1)S(1)} collective-permute-done((bf16[256,512]{1,0:T(8,128)(2,1)S(1)}, bf16[256,512]{1,0:T(8,128)(2,1)S(1)}, u32[]{:S(2)}, u32[]{:S(2)}) %collective-permute-start.15) | collective-permute-done | bytes 262176 | tf_op jit(solution)/shard_map/ppermute | solution.py:481
  254.0 1.8 select_convert_fusion
  255.9 2.7 %fusion.34 = (f32[512,512]{1,0:T(8,128)}, f32[512,512]{1,0:T(8,128)}, f32[512,512]{1,0:T(8,128)}, f32[512,512]{1,0:T(8,128)}, f32[512,512]{1,0:T(8,128)}, /*index=5*/f32[512,512]{1,0:T(8,128)}) fusion(f32[1536,512]{1,0:T(8,128)S(1)} %get-tuple-element.84, f32[1536,512]{1,0:T(8,128)S(1)} %get-tuple-element.85), kind=kLoop, calls=%fused_computation.93 | loop fusion | bytes 12582912 | tf_op jit(solution)/shard_map/slice | solution.py:605
  (92 shorter events, 23.4 us)
Async XLA Ops:
  0.6 11.5 %copy-start = (bf16[8,64,512]{2,1,0:T(8,128)(2,1)S(1)}, bf16[8,64,512]{2,1,0:T(8,128)(2,1)}, u32[]{:S(2)}) copy-start(bf16[8,64,512]{2,1,0:T(8,128)(2,1)} %param.16) | copy-start | bytes 1572868
  1.8 15.0 %copy-start.17 = (s32[1,1,256,32]{2,3,1,0:T(8,128)S(1)}, s32[1,1,256,32]{2,3,1,0:T(8,128)}, u32[]{:S(2)}) copy-start(s32[1,1,256,32]{2,3,1,0:T(8,128)} %param.26) | copy-start | bytes 98308
  1.8 9.5 %collective-permute-start = (bf16[256,512]{1,0:T(8,128)(2,1)S(1)}, bf16[256,512]{1,0:T(8,128)(2,1)S(1)}, u32[]{:S(2)}, u32[]{:S(2)}) collective-permute-start(bf16[256,512]{1,0:T(8,128)(2,1)S(1)} %bitcast.66), channel_id=1, source_target_pairs={{8,0},{16,8},{24,16},{32,24},{40,32},{48,40},{56,48},{64,56},{72,6... | collective-permute-start | bytes 786440 | tf_op jit(solution)/shard_map/ppermute | solution.py:481
  3.1 9.0 %collective-permute-start.1 = (bf16[256,512]{1,0:T(8,128)(2,1)S(1)}, bf16[256,512]{1,0:T(8,128)(2,1)S(1)}, u32[]{:S(2)}, u32[]{:S(2)}) collective-permute-start(bf16[256,512]{1,0:T(8,128)(2,1)S(1)} %bitcast.65), channel_id=1, source_target_pairs={{0,8},{8,16},{16,24},{24,32},{32,40},{40,48},{48,56},{56,64},{64,7... | collective-permute-start | bytes 786440 | tf_op jit(solution)/shard_map/ppermute | solution.py:481
  11.3 8.2 %copy-start.3 = (bf16[256,512]{1,0:T(8,128)(2,1)}, bf16[256,512]{1,0:T(8,128)(2,1)S(1)}, u32[]{:S(2)}) copy-start(bf16[256,512]{1,0:T(8,128)(2,1)S(1)} %collective-permute-done.high_ref) | copy-start | bytes 786436
  12.1 7.4 %copy-start.4 = (bf16[256,512]{1,0:T(8,128)(2,1)}, bf16[256,512]{1,0:T(8,128)(2,1)S(1)}, u32[]{:S(2)}) copy-start(bf16[256,512]{1,0:T(8,128)(2,1)S(1)} %collective-permute-done.1.low_ref) | copy-start | bytes 786436
  12.3 5.3 %collective-permute-start.2 = (bf16[64,512]{1,0:T(8,128)(2,1)S(1)}, bf16[64,512]{1,0:T(8,128)(2,1)S(1)}, u32[]{:S(2)}, u32[]{:S(2)}) collective-permute-start(bf16[64,512]{1,0:T(8,128)(2,1)S(1)} %reshape.154), channel_id=1, source_target_pairs={{0,1},{1,2},{2,3},{3,4},{4,5},{5,6},{6,7},{7,0},{8,9},{9,10},{10,1... | collective-permute-start | bytes 196616 | tf_op jit(solution)/shard_map/ppermute | solution.py:476
  15.8 3.7 %collective-permute-start.3 = (bf16[64,512]{1,0:T(8,128)(2,1)S(1)}, bf16[64,512]{1,0:T(8,128)(2,1)S(1)}, u32[]{:S(2)}, u32[]{:S(2)}) collective-permute-start(bf16[64,512]{1,0:T(8,128)(2,1)S(1)} %reshape.155), channel_id=1, source_target_pairs={{0,7},{1,0},{2,1},{3,2},{4,3},{5,4},{6,5},{7,6},{8,15},{9,8},{10,9... | collective-permute-start | bytes 196616 | tf_op jit(solution)/shard_map/ppermute | solution.py:476
  46.2 12.9 %copy-start.18 = (s32[3,8,64]{2,1,0:T(8,128)S(1)}, s32[3,8,64]{2,1,0:T(8,128)}, u32[]{:S(2)}) copy-start(s32[3,8,64]{2,1,0:T(8,128)} %param.27) | copy-start | bytes 18436
  46.2 11.1 %collective-permute-start.4 = (bf16[256,512]{1,0:T(8,128)(2,1)}, bf16[256,512]{1,0:T(8,128)(2,1)S(1)}, u32[]{:S(2)}, u32[]{:S(2)}) collective-permute-start(bf16[256,512]{1,0:T(8,128)(2,1)} %get-tuple-element.56), channel_id=1, source_target_pairs={{8,0},{16,8},{24,16},{32,24},{40,32},{48,40},{56,48},{64,56},{72,6... | collective-permute-start | bytes 786440 | tf_op jit(solution)/shard_map/ppermute | solution.py:481
  47.5 10.9 %collective-permute-start.5 = (bf16[256,512]{1,0:T(8,128)(2,1)}, bf16[256,512]{1,0:T(8,128)(2,1)S(1)}, u32[]{:S(2)}, u32[]{:S(2)}) collective-permute-start(bf16[256,512]{1,0:T(8,128)(2,1)} %get-tuple-element.56), channel_id=1, source_target_pairs={{0,8},{8,16},{16,24},{24,32},{32,40},{40,48},{48,56},{56,64},{64,7... | collective-permute-start | bytes 786440 | tf_op jit(solution)/shard_map/ppermute | solution.py:481
  58.5 12.2 %copy-start.8 = (bf16[768,512]{1,0:T(8,128)(2,1)}, bf16[768,512]{1,0:T(8,128)(2,1)S(1)}, u32[]{:S(2)}) copy-start(bf16[768,512]{1,0:T(8,128)(2,1)S(1)} %constant_dynamic-update-slice_fusion.centre_ref) | copy-start | bytes 2359300
  58.5 9.4 %collective-permute-start.6 = (bf16[768,512]{1,0:T(8,128)(2,1)S(1)}, bf16[768,512]{1,0:T(8,128)(2,1)S(1)}, u32[]{:S(2)}, u32[]{:S(2)}) collective-permute-start(bf16[768,512]{1,0:T(8,128)(2,1)S(1)} %constant_dynamic-update-slice_fusion.centre_ref), channel_id=1, source_target_pairs={{0,1},{1,2},{2,3},{3,4},{4,5},{5,6},{6,7},{7,0},{8,9},{9,10},{10,1... | collective-permute-start | bytes 2359304 | tf_op jit(solution)/shard_map/ppermute | solution.py:476
  58.9 11.7 %collective-permute-start.7 = (bf16[768,512]{1,0:T(8,128)(2,1)S(1)}, bf16[768,512]{1,0:T(8,128)(2,1)S(1)}, u32[]{:S(2)}, u32[]{:S(2)}) collective-permute-start(bf16[768,512]{1,0:T(8,128)(2,1)S(1)} %constant_dynamic-update-slice_fusion.centre_ref), channel_id=1, source_target_pairs={{0,7},{1,0},{2,1},{3,2},{4,3},{5,4},{6,5},{7,6},{8,15},{9,8},{10,9... | collective-permute-start | bytes 2359304 | tf_op jit(solution)/shard_map/ppermute | solution.py:476
  71.5 14.4 %copy-start.16 = (s32[1,1,256,32]{2,3,1,0:T(8,128)S(1)}, s32[1,1,256,32]{2,3,1,0:T(8,128)}, u32[]{:S(2)}) copy-start(s32[1,1,256,32]{2,3,1,0:T(8,128)} %param.25) | copy-start | bytes 98308
  84.2 11.9 %collective-permute-start.8 = (bf16[768,512]{1,0:T(8,128)(2,1)}, bf16[768,512]{1,0:T(8,128)(2,1)S(1)}, u32[]{:S(2)}, u32[]{:S(2)}) collective-permute-start(bf16[768,512]{1,0:T(8,128)(2,1)} %get-tuple-element.64), channel_id=1, source_target_pairs={{0,7},{1,0},{2,1},{3,2},{4,3},{5,4},{6,5},{7,6},{8,15},{9,8},{10,9... | collective-permute-start | bytes 2359304 | tf_op jit(solution)/shard_map/ppermute | solution.py:476
  85.6 10.5 %collective-permute-start.9 = (bf16[768,512]{1,0:T(8,128)(2,1)}, bf16[768,512]{1,0:T(8,128)(2,1)S(1)}, u32[]{:S(2)}, u32[]{:S(2)}) collective-permute-start(bf16[768,512]{1,0:T(8,128)(2,1)} %get-tuple-element.65), channel_id=1, source_target_pairs={{0,1},{1,2},{2,3},{3,4},{4,5},{5,6},{6,7},{7,0},{8,9},{9,10},{10,1... | collective-permute-start | bytes 2359304 | tf_op jit(solution)/shard_map/ppermute | solution.py:476
  97.7 28.1 %collective-permute-start.10 = (bf16[256,512]{1,0:T(8,128)(2,1)S(1)}, bf16[256,512]{1,0:T(8,128)(2,1)S(1)}, u32[]{:S(2)}, u32[]{:S(2)}) collective-permute-start(bf16[256,512]{1,0:T(8,128)(2,1)S(1)} %get-tuple-element.95), channel_id=1, source_target_pairs={{0,8},{8,16},{16,24},{24,32},{32,40},{40,48},{48,56},{56,64},{64,7... | collective-permute-start | bytes 786440 | tf_op jit(solution)/shard_map/ppermute | solution.py:481
  101.7 24.1 %collective-permute-start.11 = (bf16[256,512]{1,0:T(8,128)(2,1)S(1)}, bf16[256,512]{1,0:T(8,128)(2,1)S(1)}, u32[]{:S(2)}, u32[]{:S(2)}) collective-permute-start(bf16[256,512]{1,0:T(8,128)(2,1)S(1)} %get-tuple-element.96), channel_id=1, source_target_pairs={{8,0},{16,8},{24,16},{32,24},{40,32},{48,40},{56,48},{64,56},{72,6... | collective-permute-start | bytes 786440 | tf_op jit(solution)/shard_map/ppermute | solution.py:481
  103.0 22.9 %copy-start.15 = (bf16[256,512]{1,0:T(8,128)(2,1)S(1)}, bf16[256,512]{1,0:T(8,128)(2,1)}, u32[]{:S(2)}) copy-start(bf16[256,512]{1,0:T(8,128)(2,1)} %get-tuple-element.76) | copy-start | bytes 786436
  126.6 31.6 %copy-start.5 = (bf16[512,512]{1,0:T(8,128)(2,1)S(1)}, bf16[512,512]{1,0:T(8,128)(2,1)}, u32[]{:S(2)}) copy-start(bf16[512,512]{1,0:T(8,128)(2,1)} %get-tuple-element.78) | copy-start | bytes 1572868
  126.6 31.6 %copy-start.6 = (bf16[512,512]{1,0:T(8,128)(2,1)S(1)}, bf16[512,512]{1,0:T(8,128)(2,1)}, u32[]{:S(2)}) copy-start(bf16[512,512]{1,0:T(8,128)(2,1)} %get-tuple-element.77) | copy-start | bytes 1572868
  158.2 9.1 %copy-start.1 = (bf16[1536,512]{1,0:T(8,128)(2,1)S(1)}, bf16[1536,512]{1,0:T(8,128)(2,1)}, u32[]{:S(2)}) copy-start(bf16[1536,512]{1,0:T(8,128)(2,1)} %get-tuple-element.75) | copy-start | bytes 4718596
  160.2 7.1 %collective-permute-start.16 = (bf16[1536,512]{1,0:T(8,128)(2,1)S(1)}, bf16[1536,512]{1,0:T(8,128)(2,1)S(1)}, u32[]{:S(2)}, u32[]{:S(2)}) collective-permute-start(bf16[1536,512]{1,0:T(8,128)(2,1)S(1)} %broadcast_select_fusion), channel_id=1, source_target_pairs={{0,1},{1,0},{2,3},{3,2},{4,5},{5,4},{6,7},{7,6},{8,9},{9,8},{10,11... | collective-permute-start | bytes 4718600 | tf_op jit(solution)/shard_map/ppermute | solution.py:493
  208.7 6.0 %copy-start.9 = (bf16[1152,512]{1,0:T(8,128)(2,1)S(1)}, bf16[1152,512]{1,0:T(8,128)(2,1)}, u32[]{:S(2)}) copy-start(bf16[1152,512]{1,0:T(8,128)(2,1)} %get-tuple-element.73) | copy-start | bytes 3538948
  208.7 27.8 %all-to-all-start.1 = ((bf16[64,24,512]{2,1,0:T(8,128)(2,1)}), bf16[64,24,512]{2,1,0:T(8,128)(2,1)}, u32[]{:S(2)}, u32[]{:S(2)}) async-start(bf16[64,24,512]{2,1,0:T(8,128)(2,1)} %broadcast_in_dim.12), calls=%async_computation.1 | async-start | bytes 3145728 | tf_op jit(solution)/shard_map/all_to_all | solution.py:498
  214.7 14.6 %collective-permute-start.12 = (bf16[64,512]{1,0:T(8,128)(2,1)S(1)}, bf16[64,512]{1,0:T(8,128)(2,1)S(1)}, u32[]{:S(2)}, u32[]{:S(2)}) collective-permute-start(bf16[64,512]{1,0:T(8,128)(2,1)S(1)} %get-tuple-element.90), channel_id=1, source_target_pairs={{0,7},{1,0},{2,1},{3,2},{4,3},{5,4},{6,5},{7,6},{8,15},{9,8},{10,9... | collective-permute-start | bytes 196616 | tf_op jit(solution)/shard_map/ppermute | solution.py:476
  216.7 12.7 %collective-permute-start.13 = (bf16[64,512]{1,0:T(8,128)(2,1)S(1)}, bf16[64,512]{1,0:T(8,128)(2,1)S(1)}, u32[]{:S(2)}, u32[]{:S(2)}) collective-permute-start(bf16[64,512]{1,0:T(8,128)(2,1)S(1)} %get-tuple-element.89), channel_id=1, source_target_pairs={{0,1},{1,2},{2,3},{3,4},{4,5},{5,6},{6,7},{7,0},{8,9},{9,10},{10,1... | collective-permute-start | bytes 196616 | tf_op jit(solution)/shard_map/ppermute | solution.py:476
  236.4 17.6 %collective-permute-start.17 = (bf16[1536,512]{1,0:T(8,128)(2,1)}, bf16[1536,512]{1,0:T(8,128)(2,1)S(1)}, u32[]{:S(2)}, u32[]{:S(2)}) collective-permute-start(bf16[1536,512]{1,0:T(8,128)(2,1)} %bitcast.19), channel_id=1, source_target_pairs={{0,1},{1,0},{2,3},{3,2},{4,5},{5,4},{6,7},{7,6},{8,9},{9,8},{10,11... | collective-permute-start | bytes 4718600 | tf_op jit(solution)/shard_map/ppermute | solution.py:499
  239.9 7.9 %collective-permute-start.14 = (bf16[256,512]{1,0:T(8,128)(2,1)S(1)}, bf16[256,512]{1,0:T(8,128)(2,1)S(1)}, u32[]{:S(2)}, u32[]{:S(2)}) collective-permute-start(bf16[256,512]{1,0:T(8,128)(2,1)S(1)} %bitcast.68), channel_id=1, source_target_pairs={{0,8},{8,16},{16,24},{24,32},{32,40},{40,48},{48,56},{56,64},{64,7... | collective-permute-start | bytes 786440 | tf_op jit(solution)/shard_map/ppermute | solution.py:481
  242.2 9.5 %collective-permute-start.15 = (bf16[256,512]{1,0:T(8,128)(2,1)S(1)}, bf16[256,512]{1,0:T(8,128)(2,1)S(1)}, u32[]{:S(2)}, u32[]{:S(2)}) collective-permute-start(bf16[256,512]{1,0:T(8,128)(2,1)S(1)} %bitcast.67), channel_id=1, source_target_pairs={{8,0},{16,8},{24,16},{32,24},{40,32},{48,40},{56,48},{64,56},{72,6... | collective-permute-start | bytes 786440 | tf_op jit(solution)/shard_map/ppermute | solution.py:481
  243.5 8.3 %copy-start.7 = (bf16[512,512]{1,0:T(8,128)(2,1)S(1)}, bf16[512,512]{1,0:T(8,128)(2,1)}, u32[]{:S(2)}) copy-start(bf16[512,512]{1,0:T(8,128)(2,1)} %send_ref.1) | copy-start | bytes 1572868
  (6 other events, 8.1 us)
